TPU v7x, 1024 devices: a whole 4x8x16 slice. The times are simulated.
1024 devices in a mesh: blk: 16 (over y_hi, x), dp: 64 (over z, y_lo, core).
Axes of the slice: x: 4, y: 8 (y_hi: 4, y_lo: 2; y = y_hi * 2 + y_lo), z: 16, core: 2. Of those that a mesh axis runs over, the one named last changes fastest.
Arguments:
- image_embeddings: bfloat16 [196608, 640], P(('dp', 'blk')), parts along dimension 0, may hold values from -0.23632812 to 0.23632812
- text_embeddings: bfloat16 [196608, 640], P(('dp', 'blk')), parts along dimension 0, may hold values from -0.23632812 to 0.23632812
- pair_labels: int32 [196608], P(('dp', 'blk')), parts along dimension 0, may hold values from 0 to 3071, as said below
Outputs:
- image_grads: float32 [196608, 640], P(('dp', 'blk')), parts along dimension 0
- text_grads: float32 [196608, 640], P(('dp', 'blk')), parts along dimension 0
There are 64 independent parts, one for each index of `dp`. A program takes and returns all parts, laid end to end along the dimension named above; each array names one. Nothing has to cross between parts.
Inputs may be any that keep to these rules, and one draw needn't show every extreme that they name: pair_labels is a permutation: every text row is paired with exactly one image row.
All inputs are finite; a program needn't handle non-finite values.
Results may differ from a plain program's by a relative error of at most 0.002.
Values may be sent and summed in bfloat16 or wider, within the bound.
No kernel may reach another device: no remote copies, remote signals or barrier semaphores. Data moves between devices by JAX's collectives and lax.ppermute only.
A program may use at most 32 MiB of HBM per device.

v0:
```python
import jax
import jax.numpy as jnp
from jax import lax
from jax.sharding import PartitionSpec as P

logit_scale = 25.0
logit_bias = -1.0


def shifted(value, axis, steps):
    count = lax.axis_size(axis)
    pairs = [(source, (source + steps) % count) for source in range(count)]
    return lax.ppermute(value, axis, pairs)


def coefficients(image_rows, labels, text_piece, first, blocks):
    logits = (
        logit_scale
        * lax.dot_general(
            image_rows, text_piece, (((1,), (1,)), ((), ())), preferred_element_type=jnp.float32
        )
        + logit_bias
    )
    columns = first + lax.broadcasted_iota(jnp.int32, logits.shape, 1)
    signs = jnp.where(labels[:, None] == columns, jnp.float32(1.0), jnp.float32(-1.0))
    return (-signs * jax.nn.sigmoid(-signs * logits) / blocks).astype(jnp.bfloat16)


def image_term(coeff, text_piece):
    return logit_scale * jnp.dot(coeff, text_piece, preferred_element_type=jnp.float32)


def text_term(coeff, image_rows):
    return logit_scale * lax.dot_general(
        coeff, image_rows, (((0,), (0,)), ((), ())), preferred_element_type=jnp.float32
    )


def on_device(image_embeddings, text_embeddings, pair_labels):
    blocks = lax.axis_size("blk")
    position = lax.axis_index("blk")
    text_rows = text_embeddings.shape[0]
    width = text_embeddings.shape[1]
    scale_blocks = jnp.float32(blocks)
    own_coeff = coefficients(
        image_embeddings, pair_labels, text_embeddings, position * text_rows, scale_blocks
    )
    image_grads = image_term(own_coeff, text_embeddings)
    own_text = text_term(own_coeff, image_embeddings)

    def turn_one(turn, carry):
        current, partial_sum, image_total = carry
        current = shifted(current, "blk", 1)
        anchor = (position - turn) % blocks
        coeff = coefficients(
            image_embeddings, pair_labels, current, anchor * text_rows, scale_blocks
        )
        image_total = image_total + image_term(coeff, current)
        partial_sum = shifted(partial_sum + text_term(coeff, image_embeddings), "blk", 1)
        return (current, partial_sum, image_total)

    start = (text_embeddings, jnp.zeros((text_rows, width), jnp.float32), image_grads)
    current, partial_sum, image_grads = lax.fori_loop(1, blocks, turn_one, start)
    return (image_grads, partial_sum + own_text)


def solution(mesh):
    placed = (P(("dp", "blk"), None), P(("dp", "blk"), None), P(("dp", "blk")))
    return jax.shard_map(
        on_device,
        mesh=mesh,
        in_specs=placed,
        out_specs=(P(("dp", "blk"), None), P(("dp", "blk"), None)),
        check_vma=False,
    )
```

profile of v0, /device:TPU:264, one launch (start us, length us, event | category | flops | bytes accessed | tf_op | source)
XLA Modules:
  0.0 641.1 jit_solution(5640277851687367817)
XLA Ops:
  2.9 637.1 %while.19 = (s32[]{:T(128)}, bf16[192,640]{1,0:T(8,128)(2,1)S(1)}, f32[192,640]{1,0:T(8,128)S(1)}, f32[192,640]{1,0:T(8,128)S(1)}, s32[192]{0:T(256)S(1)}, /*ind...) while((s32[]{:T(128)}, bf16[192,640]{1,0:T(8,128)(2,1)S(1)}, ...), condition=%wide.region_1.2_spmd, body=%wide.region_0.1_spmd.sunk | while | flops 142491856 | bytes 6613582 | solution.py:63
  6.4 15.6 %collective-permute-done = bf16[192,640]{1,0:T(8,128)(2,1)S(1)} collective-permute-done((bf16[192,640]{1,0:T(8,128)(2,1)S(1)}, bf16[192,640]{1,0:T(8,128)(2,1)S(1)}, u32[]{:S(2)}, u32[]{:S(2)}) %collective-permute-start) | collective-permute-done | bytes 245792 | tf_op jit(solution)/shard_map/while/body/eval_jaxpr/ppermute | solution.py:13
  24.8 24.6 %collective-permute-done.1 = f32[192,640]{1,0:T(8,128)S(1)} collective-permute-done((f32[192,640]{1,0:T(8,128)S(1)}, f32[192,640]{1,0:T(8,128)S(1)}, u32[]{:S(2)}, u32[]{:S(2)}) %collective-permute-start.1) | collective-permute-done | bytes 491552 | tf_op jit(solution)/shard_map/while/body/eval_jaxpr/ppermute | solution.py:13
  51.4 19.3 %collective-permute-done = bf16[192,640]{1,0:T(8,128)(2,1)S(1)} collective-permute-done((bf16[192,640]{1,0:T(8,128)(2,1)S(1)}, bf16[192,640]{1,0:T(8,128)(2,1)S(1)}, u32[]{:S(2)}, u32[]{:S(2)}) %collective-permute-start) | collective-permute-done | bytes 245792 | tf_op jit(solution)/shard_map/while/body/eval_jaxpr/ppermute | solution.py:13
  73.5 21.5 %collective-permute-done.1 = f32[192,640]{1,0:T(8,128)S(1)} collective-permute-done((f32[192,640]{1,0:T(8,128)S(1)}, f32[192,640]{1,0:T(8,128)S(1)}, u32[]{:S(2)}, u32[]{:S(2)}) %collective-permute-start.1) | collective-permute-done | bytes 491552 | tf_op jit(solution)/shard_map/while/body/eval_jaxpr/ppermute | solution.py:13
  113.3 27.4 %collective-permute-done.1 = f32[192,640]{1,0:T(8,128)S(1)} collective-permute-done((f32[192,640]{1,0:T(8,128)S(1)}, f32[192,640]{1,0:T(8,128)S(1)}, u32[]{:S(2)}, u32[]{:S(2)}) %collective-permute-start.1) | collective-permute-done | bytes 491552 | tf_op jit(solution)/shard_map/while/body/eval_jaxpr/ppermute | solution.py:13
  142.6 13.7 %collective-permute-done = bf16[192,640]{1,0:T(8,128)(2,1)S(1)} collective-permute-done((bf16[192,640]{1,0:T(8,128)(2,1)S(1)}, bf16[192,640]{1,0:T(8,128)(2,1)S(1)}, u32[]{:S(2)}, u32[]{:S(2)}) %collective-permute-start) | collective-permute-done | bytes 245792 | tf_op jit(solution)/shard_map/while/body/eval_jaxpr/ppermute | solution.py:13
  159.1 19.7 %collective-permute-done.1 = f32[192,640]{1,0:T(8,128)S(1)} collective-permute-done((f32[192,640]{1,0:T(8,128)S(1)}, f32[192,640]{1,0:T(8,128)S(1)}, u32[]{:S(2)}, u32[]{:S(2)}) %collective-permute-start.1) | collective-permute-done | bytes 491552 | tf_op jit(solution)/shard_map/while/body/eval_jaxpr/ppermute | solution.py:13
  196.4 18.5 %collective-permute-done.1 = f32[192,640]{1,0:T(8,128)S(1)} collective-permute-done((f32[192,640]{1,0:T(8,128)S(1)}, f32[192,640]{1,0:T(8,128)S(1)}, u32[]{:S(2)}, u32[]{:S(2)}) %collective-permute-start.1) | collective-permute-done | bytes 491552 | tf_op jit(solution)/shard_map/while/body/eval_jaxpr/ppermute | solution.py:13
  216.9 15.7 %collective-permute-done = bf16[192,640]{1,0:T(8,128)(2,1)S(1)} collective-permute-done((bf16[192,640]{1,0:T(8,128)(2,1)S(1)}, bf16[192,640]{1,0:T(8,128)(2,1)S(1)}, u32[]{:S(2)}, u32[]{:S(2)}) %collective-permute-start) | collective-permute-done | bytes 245792 | tf_op jit(solution)/shard_map/while/body/eval_jaxpr/ppermute | solution.py:13
  235.4 25.2 %collective-permute-done.1 = f32[192,640]{1,0:T(8,128)S(1)} collective-permute-done((f32[192,640]{1,0:T(8,128)S(1)}, f32[192,640]{1,0:T(8,128)S(1)}, u32[]{:S(2)}, u32[]{:S(2)}) %collective-permute-start.1) | collective-permute-done | bytes 491552 | tf_op jit(solution)/shard_map/while/body/eval_jaxpr/ppermute | solution.py:13
  262.6 17.6 %collective-permute-done = bf16[192,640]{1,0:T(8,128)(2,1)S(1)} collective-permute-done((bf16[192,640]{1,0:T(8,128)(2,1)S(1)}, bf16[192,640]{1,0:T(8,128)(2,1)S(1)}, u32[]{:S(2)}, u32[]{:S(2)}) %collective-permute-start) | collective-permute-done | bytes 245792 | tf_op jit(solution)/shard_map/while/body/eval_jaxpr/ppermute | solution.py:13
  283.0 23.3 %collective-permute-done.1 = f32[192,640]{1,0:T(8,128)S(1)} collective-permute-done((f32[192,640]{1,0:T(8,128)S(1)}, f32[192,640]{1,0:T(8,128)S(1)}, u32[]{:S(2)}, u32[]{:S(2)}) %collective-permute-start.1) | collective-permute-done | bytes 491552 | tf_op jit(solution)/shard_map/while/body/eval_jaxpr/ppermute | solution.py:13
  323.3 25.6 %collective-permute-done.1 = f32[192,640]{1,0:T(8,128)S(1)} collective-permute-done((f32[192,640]{1,0:T(8,128)S(1)}, f32[192,640]{1,0:T(8,128)S(1)}, u32[]{:S(2)}, u32[]{:S(2)}) %collective-permute-start.1) | collective-permute-done | bytes 491552 | tf_op jit(solution)/shard_map/while/body/eval_jaxpr/ppermute | solution.py:13
  365.7 23.4 %collective-permute-done.1 = f32[192,640]{1,0:T(8,128)S(1)} collective-permute-done((f32[192,640]{1,0:T(8,128)S(1)}, f32[192,640]{1,0:T(8,128)S(1)}, u32[]{:S(2)}, u32[]{:S(2)}) %collective-permute-start.1) | collective-permute-done | bytes 491552 | tf_op jit(solution)/shard_map/while/body/eval_jaxpr/ppermute | solution.py:13
  391.0 13.8 %collective-permute-done = bf16[192,640]{1,0:T(8,128)(2,1)S(1)} collective-permute-done((bf16[192,640]{1,0:T(8,128)(2,1)S(1)}, bf16[192,640]{1,0:T(8,128)(2,1)S(1)}, u32[]{:S(2)}, u32[]{:S(2)}) %collective-permute-start) | collective-permute-done | bytes 245792 | tf_op jit(solution)/shard_map/while/body/eval_jaxpr/ppermute | solution.py:13
  407.7 22.1 %collective-permute-done.1 = f32[192,640]{1,0:T(8,128)S(1)} collective-permute-done((f32[192,640]{1,0:T(8,128)S(1)}, f32[192,640]{1,0:T(8,128)S(1)}, u32[]{:S(2)}, u32[]{:S(2)}) %collective-permute-start.1) | collective-permute-done | bytes 491552 | tf_op jit(solution)/shard_map/while/body/eval_jaxpr/ppermute | solution.py:13
  431.7 16.3 %collective-permute-done = bf16[192,640]{1,0:T(8,128)(2,1)S(1)} collective-permute-done((bf16[192,640]{1,0:T(8,128)(2,1)S(1)}, bf16[192,640]{1,0:T(8,128)(2,1)S(1)}, u32[]{:S(2)}, u32[]{:S(2)}) %collective-permute-start) | collective-permute-done | bytes 245792 | tf_op jit(solution)/shard_map/while/body/eval_jaxpr/ppermute | solution.py:13
  450.8 25.5 %collective-permute-done.1 = f32[192,640]{1,0:T(8,128)S(1)} collective-permute-done((f32[192,640]{1,0:T(8,128)S(1)}, f32[192,640]{1,0:T(8,128)S(1)}, u32[]{:S(2)}, u32[]{:S(2)}) %collective-permute-start.1) | collective-permute-done | bytes 491552 | tf_op jit(solution)/shard_map/while/body/eval_jaxpr/ppermute | solution.py:13
  478.2 14.6 %collective-permute-done = bf16[192,640]{1,0:T(8,128)(2,1)S(1)} collective-permute-done((bf16[192,640]{1,0:T(8,128)(2,1)S(1)}, bf16[192,640]{1,0:T(8,128)(2,1)S(1)}, u32[]{:S(2)}, u32[]{:S(2)}) %collective-permute-start) | collective-permute-done | bytes 245792 | tf_op jit(solution)/shard_map/while/body/eval_jaxpr/ppermute | solution.py:13
  495.6 32.7 %collective-permute-done.1 = f32[192,640]{1,0:T(8,128)S(1)} collective-permute-done((f32[192,640]{1,0:T(8,128)S(1)}, f32[192,640]{1,0:T(8,128)S(1)}, u32[]{:S(2)}, u32[]{:S(2)}) %collective-permute-start.1) | collective-permute-done | bytes 491552 | tf_op jit(solution)/shard_map/while/body/eval_jaxpr/ppermute | solution.py:13
  530.2 20.4 %collective-permute-done = bf16[192,640]{1,0:T(8,128)(2,1)S(1)} collective-permute-done((bf16[192,640]{1,0:T(8,128)(2,1)S(1)}, bf16[192,640]{1,0:T(8,128)(2,1)S(1)}, u32[]{:S(2)}, u32[]{:S(2)}) %collective-permute-start) | collective-permute-done | bytes 245792 | tf_op jit(solution)/shard_map/while/body/eval_jaxpr/ppermute | solution.py:13
  553.5 20.3 %collective-permute-done.1 = f32[192,640]{1,0:T(8,128)S(1)} collective-permute-done((f32[192,640]{1,0:T(8,128)S(1)}, f32[192,640]{1,0:T(8,128)S(1)}, u32[]{:S(2)}, u32[]{:S(2)}) %collective-permute-start.1) | collective-permute-done | bytes 491552 | tf_op jit(solution)/shard_map/while/body/eval_jaxpr/ppermute | solution.py:13
  575.7 20.9 %collective-permute-done = bf16[192,640]{1,0:T(8,128)(2,1)S(1)} collective-permute-done((bf16[192,640]{1,0:T(8,128)(2,1)S(1)}, bf16[192,640]{1,0:T(8,128)(2,1)S(1)}, u32[]{:S(2)}, u32[]{:S(2)}) %collective-permute-start) | collective-permute-done | bytes 245792 | tf_op jit(solution)/shard_map/while/body/eval_jaxpr/ppermute | solution.py:13
  (124 shorter events, 161.6 us)
Async XLA Ops:
  2.9 19.1 %collective-permute-start = (bf16[192,640]{1,0:T(8,128)(2,1)S(1)}, bf16[192,640]{1,0:T(8,128)(2,1)S(1)}, u32[]{:S(2)}, u32[]{:S(2)}) collective-permute-start(bf16[192,640]{1,0:T(8,128)(2,1)S(1)} %get-tuple-element.252), channel_id=1, source_target_pairs={{0,64},{64,128},{128,192},{192,256},{256,320},{320,384},{384,448},... | collective-permute-start | bytes 737288 | tf_op jit(solution)/shard_map/while/body/eval_jaxpr/ppermute | solution.py:13
  22.6 26.9 %collective-permute-start.1 = (f32[192,640]{1,0:T(8,128)S(1)}, f32[192,640]{1,0:T(8,128)S(1)}, u32[]{:S(2)}, u32[]{:S(2)}) collective-permute-start(f32[192,640]{1,0:T(8,128)S(1)} %fusion.49), channel_id=1, source_target_pairs={{0,64},{64,128},{128,192},{192,256},{256,320},{320,384},{384,448},... | collective-permute-start | bytes 1474568 | tf_op jit(solution)/shard_map/while/body/eval_jaxpr/ppermute | solution.py:13
  49.5 21.3 %collective-permute-start = (bf16[192,640]{1,0:T(8,128)(2,1)S(1)}, bf16[192,640]{1,0:T(8,128)(2,1)S(1)}, u32[]{:S(2)}, u32[]{:S(2)}) collective-permute-start(bf16[192,640]{1,0:T(8,128)(2,1)S(1)} %get-tuple-element.252), channel_id=1, source_target_pairs={{0,64},{64,128},{128,192},{192,256},{256,320},{320,384},{384,448},... | collective-permute-start | bytes 737288 | tf_op jit(solution)/shard_map/while/body/eval_jaxpr/ppermute | solution.py:13
  71.3 23.7 %collective-permute-start.1 = (f32[192,640]{1,0:T(8,128)S(1)}, f32[192,640]{1,0:T(8,128)S(1)}, u32[]{:S(2)}, u32[]{:S(2)}) collective-permute-start(f32[192,640]{1,0:T(8,128)S(1)} %fusion.49), channel_id=1, source_target_pairs={{0,64},{64,128},{128,192},{192,256},{256,320},{320,384},{384,448},... | collective-permute-start | bytes 1474568 | tf_op jit(solution)/shard_map/while/body/eval_jaxpr/ppermute | solution.py:13
  95.1 15.4 %collective-permute-start = (bf16[192,640]{1,0:T(8,128)(2,1)S(1)}, bf16[192,640]{1,0:T(8,128)(2,1)S(1)}, u32[]{:S(2)}, u32[]{:S(2)}) collective-permute-start(bf16[192,640]{1,0:T(8,128)(2,1)S(1)} %get-tuple-element.252), channel_id=1, source_target_pairs={{0,64},{64,128},{128,192},{192,256},{256,320},{320,384},{384,448},... | collective-permute-start | bytes 737288 | tf_op jit(solution)/shard_map/while/body/eval_jaxpr/ppermute | solution.py:13
  111.1 29.6 %collective-permute-start.1 = (f32[192,640]{1,0:T(8,128)S(1)}, f32[192,640]{1,0:T(8,128)S(1)}, u32[]{:S(2)}, u32[]{:S(2)}) collective-permute-start(f32[192,640]{1,0:T(8,128)S(1)} %fusion.49), channel_id=1, source_target_pairs={{0,64},{64,128},{128,192},{192,256},{256,320},{320,384},{384,448},... | collective-permute-start | bytes 1474568 | tf_op jit(solution)/shard_map/while/body/eval_jaxpr/ppermute | solution.py:13
  140.7 15.6 %collective-permute-start = (bf16[192,640]{1,0:T(8,128)(2,1)S(1)}, bf16[192,640]{1,0:T(8,128)(2,1)S(1)}, u32[]{:S(2)}, u32[]{:S(2)}) collective-permute-start(bf16[192,640]{1,0:T(8,128)(2,1)S(1)} %get-tuple-element.252), channel_id=1, source_target_pairs={{0,64},{64,128},{128,192},{192,256},{256,320},{320,384},{384,448},... | collective-permute-start | bytes 737288 | tf_op jit(solution)/shard_map/while/body/eval_jaxpr/ppermute | solution.py:13
  156.9 21.9 %collective-permute-start.1 = (f32[192,640]{1,0:T(8,128)S(1)}, f32[192,640]{1,0:T(8,128)S(1)}, u32[]{:S(2)}, u32[]{:S(2)}) collective-permute-start(f32[192,640]{1,0:T(8,128)S(1)} %fusion.49), channel_id=1, source_target_pairs={{0,64},{64,128},{128,192},{192,256},{256,320},{320,384},{384,448},... | collective-permute-start | bytes 1474568 | tf_op jit(solution)/shard_map/while/body/eval_jaxpr/ppermute | solution.py:13
  194.2 20.7 %collective-permute-start.1 = (f32[192,640]{1,0:T(8,128)S(1)}, f32[192,640]{1,0:T(8,128)S(1)}, u32[]{:S(2)}, u32[]{:S(2)}) collective-permute-start(f32[192,640]{1,0:T(8,128)S(1)} %fusion.49), channel_id=1, source_target_pairs={{0,64},{64,128},{128,192},{192,256},{256,320},{320,384},{384,448},... | collective-permute-start | bytes 1474568 | tf_op jit(solution)/shard_map/while/body/eval_jaxpr/ppermute | solution.py:13
  215.0 17.6 %collective-permute-start = (bf16[192,640]{1,0:T(8,128)(2,1)S(1)}, bf16[192,640]{1,0:T(8,128)(2,1)S(1)}, u32[]{:S(2)}, u32[]{:S(2)}) collective-permute-start(bf16[192,640]{1,0:T(8,128)(2,1)S(1)} %get-tuple-element.252), channel_id=1, source_target_pairs={{0,64},{64,128},{128,192},{192,256},{256,320},{320,384},{384,448},... | collective-permute-start | bytes 737288 | tf_op jit(solution)/shard_map/while/body/eval_jaxpr/ppermute | solution.py:13
  233.2 27.4 %collective-permute-start.1 = (f32[192,640]{1,0:T(8,128)S(1)}, f32[192,640]{1,0:T(8,128)S(1)}, u32[]{:S(2)}, u32[]{:S(2)}) collective-permute-start(f32[192,640]{1,0:T(8,128)S(1)} %fusion.49), channel_id=1, source_target_pairs={{0,64},{64,128},{128,192},{192,256},{256,320},{320,384},{384,448},... | collective-permute-start | bytes 1474568 | tf_op jit(solution)/shard_map/while/body/eval_jaxpr/ppermute | solution.py:13
  260.6 19.6 %collective-permute-start = (bf16[192,640]{1,0:T(8,128)(2,1)S(1)}, bf16[192,640]{1,0:T(8,128)(2,1)S(1)}, u32[]{:S(2)}, u32[]{:S(2)}) collective-permute-start(bf16[192,640]{1,0:T(8,128)(2,1)S(1)} %get-tuple-element.252), channel_id=1, source_target_pairs={{0,64},{64,128},{128,192},{192,256},{256,320},{320,384},{384,448},... | collective-permute-start | bytes 737288 | tf_op jit(solution)/shard_map/while/body/eval_jaxpr/ppermute | solution.py:13
  280.8 25.5 %collective-permute-start.1 = (f32[192,640]{1,0:T(8,128)S(1)}, f32[192,640]{1,0:T(8,128)S(1)}, u32[]{:S(2)}, u32[]{:S(2)}) collective-permute-start(f32[192,640]{1,0:T(8,128)S(1)} %fusion.49), channel_id=1, source_target_pairs={{0,64},{64,128},{128,192},{192,256},{256,320},{320,384},{384,448},... | collective-permute-start | bytes 1474568 | tf_op jit(solution)/shard_map/while/body/eval_jaxpr/ppermute | solution.py:13
  321.1 27.8 %collective-permute-start.1 = (f32[192,640]{1,0:T(8,128)S(1)}, f32[192,640]{1,0:T(8,128)S(1)}, u32[]{:S(2)}, u32[]{:S(2)}) collective-permute-start(f32[192,640]{1,0:T(8,128)S(1)} %fusion.49), channel_id=1, source_target_pairs={{0,64},{64,128},{128,192},{192,256},{256,320},{320,384},{384,448},... | collective-permute-start | bytes 1474568 | tf_op jit(solution)/shard_map/while/body/eval_jaxpr/ppermute | solution.py:13
  363.5 25.6 %collective-permute-start.1 = (f32[192,640]{1,0:T(8,128)S(1)}, f32[192,640]{1,0:T(8,128)S(1)}, u32[]{:S(2)}, u32[]{:S(2)}) collective-permute-start(f32[192,640]{1,0:T(8,128)S(1)} %fusion.49), channel_id=1, source_target_pairs={{0,64},{64,128},{128,192},{192,256},{256,320},{320,384},{384,448},... | collective-permute-start | bytes 1474568 | tf_op jit(solution)/shard_map/while/body/eval_jaxpr/ppermute | solution.py:13
  389.1 15.8 %collective-permute-start = (bf16[192,640]{1,0:T(8,128)(2,1)S(1)}, bf16[192,640]{1,0:T(8,128)(2,1)S(1)}, u32[]{:S(2)}, u32[]{:S(2)}) collective-permute-start(bf16[192,640]{1,0:T(8,128)(2,1)S(1)} %get-tuple-element.252), channel_id=1, source_target_pairs={{0,64},{64,128},{128,192},{192,256},{256,320},{320,384},{384,448},... | collective-permute-start | bytes 737288 | tf_op jit(solution)/shard_map/while/body/eval_jaxpr/ppermute | solution.py:13
  405.4 24.3 %collective-permute-start.1 = (f32[192,640]{1,0:T(8,128)S(1)}, f32[192,640]{1,0:T(8,128)S(1)}, u32[]{:S(2)}, u32[]{:S(2)}) collective-permute-start(f32[192,640]{1,0:T(8,128)S(1)} %fusion.49), channel_id=1, source_target_pairs={{0,64},{64,128},{128,192},{192,256},{256,320},{320,384},{384,448},... | collective-permute-start | bytes 1474568 | tf_op jit(solution)/shard_map/while/body/eval_jaxpr/ppermute | solution.py:13
  429.7 18.2 %collective-permute-start = (bf16[192,640]{1,0:T(8,128)(2,1)S(1)}, bf16[192,640]{1,0:T(8,128)(2,1)S(1)}, u32[]{:S(2)}, u32[]{:S(2)}) collective-permute-start(bf16[192,640]{1,0:T(8,128)(2,1)S(1)} %get-tuple-element.252), channel_id=1, source_target_pairs={{0,64},{64,128},{128,192},{192,256},{256,320},{320,384},{384,448},... | collective-permute-start | bytes 737288 | tf_op jit(solution)/shard_map/while/body/eval_jaxpr/ppermute | solution.py:13
  448.6 27.7 %collective-permute-start.1 = (f32[192,640]{1,0:T(8,128)S(1)}, f32[192,640]{1,0:T(8,128)S(1)}, u32[]{:S(2)}, u32[]{:S(2)}) collective-permute-start(f32[192,640]{1,0:T(8,128)S(1)} %fusion.49), channel_id=1, source_target_pairs={{0,64},{64,128},{128,192},{192,256},{256,320},{320,384},{384,448},... | collective-permute-start | bytes 1474568 | tf_op jit(solution)/shard_map/while/body/eval_jaxpr/ppermute | solution.py:13
  476.3 16.6 %collective-permute-start = (bf16[192,640]{1,0:T(8,128)(2,1)S(1)}, bf16[192,640]{1,0:T(8,128)(2,1)S(1)}, u32[]{:S(2)}, u32[]{:S(2)}) collective-permute-start(bf16[192,640]{1,0:T(8,128)(2,1)S(1)} %get-tuple-element.252), channel_id=1, source_target_pairs={{0,64},{64,128},{128,192},{192,256},{256,320},{320,384},{384,448},... | collective-permute-start | bytes 737288 | tf_op jit(solution)/shard_map/while/body/eval_jaxpr/ppermute | solution.py:13
  493.4 34.9 %collective-permute-start.1 = (f32[192,640]{1,0:T(8,128)S(1)}, f32[192,640]{1,0:T(8,128)S(1)}, u32[]{:S(2)}, u32[]{:S(2)}) collective-permute-start(f32[192,640]{1,0:T(8,128)S(1)} %fusion.49), channel_id=1, source_target_pairs={{0,64},{64,128},{128,192},{192,256},{256,320},{320,384},{384,448},... | collective-permute-start | bytes 1474568 | tf_op jit(solution)/shard_map/while/body/eval_jaxpr/ppermute | solution.py:13
  528.3 22.3 %collective-permute-start = (bf16[192,640]{1,0:T(8,128)(2,1)S(1)}, bf16[192,640]{1,0:T(8,128)(2,1)S(1)}, u32[]{:S(2)}, u32[]{:S(2)}) collective-permute-start(bf16[192,640]{1,0:T(8,128)(2,1)S(1)} %get-tuple-element.252), channel_id=1, source_target_pairs={{0,64},{64,128},{128,192},{192,256},{256,320},{320,384},{384,448},... | collective-permute-start | bytes 737288 | tf_op jit(solution)/shard_map/while/body/eval_jaxpr/ppermute | solution.py:13
  551.2 22.5 %collective-permute-start.1 = (f32[192,640]{1,0:T(8,128)S(1)}, f32[192,640]{1,0:T(8,128)S(1)}, u32[]{:S(2)}, u32[]{:S(2)}) collective-permute-start(f32[192,640]{1,0:T(8,128)S(1)} %fusion.49), channel_id=1, source_target_pairs={{0,64},{64,128},{128,192},{192,256},{256,320},{320,384},{384,448},... | collective-permute-start | bytes 1474568 | tf_op jit(solution)/shard_map/while/body/eval_jaxpr/ppermute | solution.py:13
  573.8 22.8 %collective-permute-start = (bf16[192,640]{1,0:T(8,128)(2,1)S(1)}, bf16[192,640]{1,0:T(8,128)(2,1)S(1)}, u32[]{:S(2)}, u32[]{:S(2)}) collective-permute-start(bf16[192,640]{1,0:T(8,128)(2,1)S(1)} %get-tuple-element.252), channel_id=1, source_target_pairs={{0,64},{64,128},{128,192},{192,256},{256,320},{320,384},{384,448},... | collective-permute-start | bytes 737288 | tf_op jit(solution)/shard_map/while/body/eval_jaxpr/ppermute | solution.py:13
  (9 other events, 88.0 us)
where the time goes:
time: 642 us; the launch traced here: 641 us
  waiting for transfers between devices  564 us (88%)
  starting transfers between devices  58.9 us (9%)
  matrix products  14.1 us (2%)
    ppermute x30, waiting for transfers between devices, shifted(): return lax.ppermute(value, axis, pairs)  564 us
    ppermute x30, starting transfers between devices, shifted(): return lax.ppermute(value, axis, pairs)  58.9 us
  transfers between devices with their start and end apart: 30, of which 30 were waited for; matrix products, arithmetic and copies ran while one was open for 1% of the time, Pallas kernels for 0%

commit v1 on v0

v1 whole, which is shorter than its diff:
```python
import functools

import jax
import jax.numpy as jnp
from jax import lax
from jax.experimental import pallas as pl
from jax.experimental.pallas import tpu as pltpu
from jax.sharding import Mesh, PartitionSpec as P

logit_scale = 25.0
logit_bias = -1.0
sides = 4
send_type = jnp.bfloat16
label_base = 64
pad_rows = 16

nt = (((1,), (1,)), ((), ()))
tn = (((0,), (0,)), ((), ()))


def shifted(value, axis, steps):
    pairs = [(source, (source + steps) % sides) for source in range(sides)]
    return lax.ppermute(value, axis, pairs)


def coefficients(text_rows, images, labels, text_ids):
    logits = (
        logit_scale
        * lax.dot_general(text_rows, images, nt, preferred_element_type=jnp.float32)
        + logit_bias
    )
    paired = labels == text_ids
    small = 1.0 / (1.0 + jnp.exp(jnp.where(paired, logits, -logits)))
    return jnp.where(paired, -small, small).astype(jnp.bfloat16)


def fill_images(bundles, images, labels):
    rows = bundles[0].shape[0] - pad_rows
    for k, bundle in enumerate(bundles):
        images[k * rows : (k + 1) * rows, :] = bundle[:rows, :]
        digits = bundle[rows:, :].astype(jnp.float32)
        labels[0:1, k * 256 : k * 256 + rows] = label_base * digits[0:1, :rows] + digits[1:2, :rows]


def near_kernel(scale, position, i0, i1, i2, i3, t0, t1, t2, own, up, down, image_part, labels_out, images_out, labs, coeff):
    rows = t0.shape[0]
    bundles = (i0, i1, i2, i3)
    for k, bundle in enumerate(bundles):
        images_out[k * rows : (k + 1) * rows, :] = bundle[:rows, :]
        digits = bundle[rows:, :].astype(jnp.float32)
        labs[k : k + 1, :] = label_base * digits[0:1, :rows] + digits[1:2, :rows]
    labels_out[...] = jnp.concatenate([labs[k : k + 1, :] for k in range(sides)], axis=1)
    total = None
    for n, (texts, out) in enumerate(((t0, own), (t1, up), (t2, down))):
        ids = position[n].astype(jnp.float32) + lax.broadcasted_iota(jnp.int32, (rows, 1), 0).astype(jnp.float32)
        c = coefficients(texts[...], images_out[...], labels_out[...], ids)
        coeff[n * rows : (n + 1) * rows, :] = c
        out[...] = (scale * jnp.dot(c, images_out[...], preferred_element_type=jnp.float32)).astype(out.dtype)
    total = None
    for n, texts in enumerate((t0, t1, t2)):
        term = lax.dot_general(coeff[n * rows : (n + 1) * rows, :], texts[...], tn, preferred_element_type=jnp.float32)
        total = term if total is None else total + term
    image_part[...] = total


def far_kernel(scale, position, texts, images, labels, image_part, far, g0, g1, g2, g3):
    rows = texts.shape[0]
    ids = position[3].astype(jnp.float32) + lax.broadcasted_iota(jnp.int32, (rows, 1), 0).astype(jnp.float32)
    c = coefficients(texts[...], images[...], labels[...], ids)
    total = scale * (image_part[...] + lax.dot_general(c, texts[...], tn, preferred_element_type=jnp.float32))
    far[...] = (scale * jnp.dot(c, images[...], preferred_element_type=jnp.float32)).astype(far.dtype)
    for k, out in enumerate((g0, g1, g2, g3)):
        out[...] = total[k * rows : (k + 1) * rows, :].astype(out.dtype)


vmem = pl.BlockSpec(memory_space=pltpu.VMEM)
smem = pl.BlockSpec(memory_space=pltpu.SMEM)
params = pltpu.CompilerParams(vmem_limit_bytes=48 * 1024 * 1024)


def on_device(image_embeddings, text_embeddings, pair_labels):
    rows, width = text_embeddings.shape
    y, x = lax.axis_index("yh"), lax.axis_index("xx")
    scale = logit_scale / (sides * sides)

    high, low = pair_labels // label_base, pair_labels % label_base
    digits = jnp.zeros((pad_rows, width), jnp.bfloat16)
    digits = digits.at[0, :rows].set(high.astype(jnp.bfloat16)).at[1, :rows].set(low.astype(jnp.bfloat16))
    bundle = jnp.concatenate([image_embeddings, digits], axis=0)

    text_up = shifted(text_embeddings, "yh", 1)
    text_down = shifted(text_embeddings, "yh", -1)
    image_1 = shifted(bundle, "xx", 1)
    image_3 = shifted(bundle, "xx", -1)
    image_2 = shifted(bundle, "xx", 2)
    text_far = shifted(text_embeddings, "yh", 2)

    owners = (y + jnp.array([0, sides - 1, 1, 2], jnp.int32)) % sides
    position = (owners * sides + x) * rows

    f32 = jnp.float32
    block = (rows, width)
    own, up, down, part, labels, images = pl.pallas_call(
        functools.partial(near_kernel, scale),
        out_shape=[
            jax.ShapeDtypeStruct(block, f32),
            jax.ShapeDtypeStruct(block, send_type),
            jax.ShapeDtypeStruct(block, send_type),
            jax.ShapeDtypeStruct((sides * rows, width), f32),
            jax.ShapeDtypeStruct((1, sides * rows), f32),
            jax.ShapeDtypeStruct((sides * rows, width), jnp.bfloat16),
        ],
        in_specs=[smem] + [vmem] * 7,
        out_specs=[vmem] * 6,
        scratch_shapes=[pltpu.VMEM((8, rows), f32), pltpu.VMEM((3 * rows, sides * rows), jnp.bfloat16)],
        compiler_params=params,
        cost_estimate=pl.CostEstimate(flops=6 * 3 * sides * rows * rows * width, bytes_accessed=6 << 20, transcendentals=0),
    )(position, bundle, image_1, image_2, image_3, text_embeddings, text_up, text_down)
    back_up = shifted(up, "yh", -1)
    back_down = shifted(down, "yh", 1)

    far, g0, g1, g2, g3 = pl.pallas_call(
        functools.partial(far_kernel, scale),
        out_shape=[jax.ShapeDtypeStruct(block, send_type), jax.ShapeDtypeStruct(block, f32)]
        + [jax.ShapeDtypeStruct(block, send_type)] * 3,
        in_specs=[smem] + [vmem] * 4,
        out_specs=[vmem] * 5,
        compiler_params=params,
        cost_estimate=pl.CostEstimate(flops=6 * sides * rows * rows * width, bytes_accessed=6 << 20, transcendentals=0),
    )(position, text_far, images, labels, part)
    back_far = shifted(far, "yh", 2)
    grad_1 = shifted(g1, "xx", -1)
    grad_3 = shifted(g3, "xx", 1)
    grad_2 = shifted(g2, "xx", 2)

    text_grads = own + back_up.astype(f32) + back_down.astype(f32) + back_far.astype(f32)
    image_grads = g0 + grad_1.astype(f32) + grad_3.astype(f32) + grad_2.astype(f32)
    return image_grads, text_grads


def solution(mesh):
    grid = Mesh(mesh.devices.reshape(sides, sides, -1), ("yh", "xx", "dp"))
    rows = P(("dp", "yh", "xx"), None)
    return jax.shard_map(
        on_device,
        mesh=grid,
        in_specs=(rows, rows, P(("dp", "yh", "xx"))),
        out_specs=(rows, rows),
        check_vma=False,
    )
```

time: 642 us -> 83.5 us (0.13)
  the two profiles are of different devices: /device:TPU:264 before, /device:TPU:4 now
where the time goes in v1:
time: 83.5 us; the launch traced here: 83 us
  starting transfers between devices  52.9 us (63%)
  waiting for transfers between devices  18.2 us (22%)
  Pallas kernels  5.75 us (7%)
  other arithmetic  4.12 us (5%)
  local copies, waits for them, and re-layouts  1.2 us (1%)
    ppermute x12, starting transfers between devices, shifted(): return lax.ppermute(value, axis, pairs)  52.9 us
    ppermute x12, waiting for transfers between devices, shifted(): return lax.ppermute(value, axis, pairs)  18.2 us
    pallas_call x1, Pallas kernels, on_device(): pl.pallas_call(functools.partial(near_kernel, scale), out_shape=[jax.Shap...  3.89 us
    pallas_call x1, Pallas kernels, on_device(): pl.pallas_call(functools.partial(far_kernel, scale), out_shape=[jax.Shape...  1.86 us
  transfers between devices with their start and end apart: 12, of which 4 were waited for; matrix products, arithmetic and copies ran while one was open for 4% of the time, Pallas kernels for 5%

profile of v1, /device:TPU:4, one launch (start us, length us, event | category | flops | bytes accessed | tf_op | source)
XLA Modules:
  0.0 83.0 jit_solution(15043984427678376449)
XLA Ops:
  0.6 4.5 %collective-permute-start.4 = (bf16[192,640]{1,0:T(8,128)(2,1)}, bf16[192,640]{1,0:T(8,128)(2,1)S(1)}, u32[]{:S(2)}, u32[]{:S(2)}) collective-permute-start(bf16[192,640]{1,0:T(8,128)(2,1)} %t0.1), channel_id=1, source_target_pairs={{0,256},{256,512},{512,768},{768,0},{1,257},{257,513},{513,769},{7... | collective-permute-start | bytes 737288 | tf_op jit(solution)/shard_map/ppermute | solution.py:23
  5.1 0.7 fusion
  6.1 1.0 %pad_maximum_fusion.i0 = bf16[208,640]{1,0:T(8,128)(2,1)S(1)} fusion(bf16[16,640]{1,0:T(8,128)(2,1)S(1)} %scatter.9, bf16[192,640]{1,0:T(8,128)(2,1)} %param.8), kind=kLoop, calls=%fused_computation.2 | loop fusion | flops 532480 | bytes 532480 | tf_op jit(solution)/shard_map/concatenate | solution.py:89
  7.1 3.1 %collective-permute-start.1 = (bf16[208,640]{1,0:T(8,128)(2,1)S(1)}, bf16[208,640]{1,0:T(8,128)(2,1)S(1)}, u32[]{:S(2)}, u32[]{:S(2)}) collective-permute-start(bf16[208,640]{1,0:T(8,128)(2,1)S(1)} %pad_maximum_fusion.i0), channel_id=1, source_target_pairs={{0,64},{64,128},{128,192},{192,0},{1,65},{65,129},{129,193},{193,1... | collective-permute-start | bytes 798728 | tf_op jit(solution)/shard_map/ppermute | solution.py:23
  10.2 11.3 %collective-permute-start.2 = (bf16[208,640]{1,0:T(8,128)(2,1)S(1)}, bf16[208,640]{1,0:T(8,128)(2,1)S(1)}, u32[]{:S(2)}, u32[]{:S(2)}) collective-permute-start(bf16[208,640]{1,0:T(8,128)(2,1)S(1)} %pad_maximum_fusion.i0), channel_id=1, source_target_pairs={{0,128},{64,192},{128,0},{192,64},{1,129},{65,193},{129,1},{193,65... | collective-permute-start | bytes 798728 | tf_op jit(solution)/shard_map/ppermute | solution.py:23
  21.5 4.5 %collective-permute-start.3 = (bf16[208,640]{1,0:T(8,128)(2,1)S(1)}, bf16[208,640]{1,0:T(8,128)(2,1)S(1)}, u32[]{:S(2)}, u32[]{:S(2)}) collective-permute-start(bf16[208,640]{1,0:T(8,128)(2,1)S(1)} %pad_maximum_fusion.i0), channel_id=1, source_target_pairs={{0,192},{64,0},{128,64},{192,128},{1,193},{65,1},{129,65},{193,129... | collective-permute-start | bytes 798728 | tf_op jit(solution)/shard_map/ppermute | solution.py:23
  26.0 6.0 %collective-permute-start.5 = (bf16[192,640]{1,0:T(8,128)(2,1)}, bf16[192,640]{1,0:T(8,128)(2,1)S(1)}, u32[]{:S(2)}, u32[]{:S(2)}) collective-permute-start(bf16[192,640]{1,0:T(8,128)(2,1)} %t0.1), channel_id=1, source_target_pairs={{0,768},{256,0},{512,256},{768,512},{1,769},{257,1},{513,257},{769... | collective-permute-start | bytes 737288 | tf_op jit(solution)/shard_map/ppermute | solution.py:23
  32.1 1.9 %collective-permute-start = (bf16[192,640]{1,0:T(8,128)(2,1)}, bf16[192,640]{1,0:T(8,128)(2,1)S(1)}, u32[]{:S(2)}, u32[]{:S(2)}) collective-permute-start(bf16[192,640]{1,0:T(8,128)(2,1)} %t0.1), channel_id=1, source_target_pairs={{0,512},{256,768},{512,0},{768,256},{1,513},{257,769},{513,1},{769... | collective-permute-start | bytes 737288 | tf_op jit(solution)/shard_map/ppermute | solution.py:23
  34.0 0.7 fusion.5.position
  34.7 3.7 %collective-permute-done.5.t2 = bf16[192,640]{1,0:T(8,128)(2,1)S(1)} collective-permute-done((bf16[192,640]{1,0:T(8,128)(2,1)}, bf16[192,640]{1,0:T(8,128)(2,1)S(1)}, u32[]{:S(2)}, u32[]{:S(2)}) %collective-permute-start.5) | collective-permute-done | bytes 245792 | tf_op jit(solution)/shard_map/ppermute | solution.py:23
  38.5 0.9 %copy-done = bf16[192,640]{1,0:T(8,128)(2,1)S(1)} copy-done((bf16[192,640]{1,0:T(8,128)(2,1)S(1)}, bf16[192,640]{1,0:T(8,128)(2,1)}, u32[]{:S(2)}) %copy-start) | copy-done | bytes 245784
  39.4 3.9 %shard_map.59 = (f32[192,640]{1,0:T(8,128)S(1)}, bf16[192,640]{1,0:T(8,128)(2,1)S(1)}, bf16[192,640]{1,0:T(8,128)(2,1)S(1)}, f32[768,640]{1,0:T(8,128)S(1)}, f32...) custom-call(s32[4]{0:T(128)S(1)} %fusion.5.position, bf16[208,640]{1,0:T(8,128)(2,1)S(1)} %pad_maximum_fusion.i0, ...), custom_call_target="tpu_custom_call" | custom-call | flops 1698693120 | bytes 6291456 | tf_op jit(solution)/shard_map/pallas_call | solution.py:103
  43.3 3.6 %collective-permute-done.texts = bf16[192,640]{1,0:T(8,128)(2,1)S(1)} collective-permute-done((bf16[192,640]{1,0:T(8,128)(2,1)}, bf16[192,640]{1,0:T(8,128)(2,1)S(1)}, u32[]{:S(2)}, u32[]{:S(2)}) %collective-permute-start) | collective-permute-done | bytes 245792 | tf_op jit(solution)/shard_map/ppermute | solution.py:23
  46.9 1.9 %shard_map.60 = (bf16[192,640]{1,0:T(8,128)(2,1)S(1)}, f32[192,640]{1,0:T(8,128)S(1)}, bf16[192,640]{1,0:T(8,128)(2,1)S(1)}, bf16[192,640]{1,0:T(8,128)(2,1)S(1)}, bf16[192,640]{1,0:T(8,128)(2,1)S(1)}) custom-call(s32[4]{0:T(128)S(1)} %fusion.5.position, bf16[192,640]{1,0:T(8,128)(2,1)S(1)} %collective-permute-done.texts, ...), custom_call_target="tpu_custom_call" | custom-call | flops 566231040 | bytes 6291456 | tf_op jit(solution)/shard_map/pallas_call | solution.py:122
  48.8 2.0 %collective-permute-start.11 = (bf16[192,640]{1,0:T(8,128)(2,1)S(1)}, bf16[192,640]{1,0:T(8,128)(2,1)S(1)}, u32[]{:S(2)}, u32[]{:S(2)}) collective-permute-start(bf16[192,640]{1,0:T(8,128)(2,1)S(1)} %get-tuple-element.47), channel_id=1, source_target_pairs={{0,512},{256,768},{512,0},{768,256},{1,513},{257,769},{513,1},{769... | collective-permute-start | bytes 737288 | tf_op jit(solution)/shard_map/ppermute | solution.py:23
  50.8 6.2 %collective-permute-start.10 = (bf16[192,640]{1,0:T(8,128)(2,1)S(1)}, bf16[192,640]{1,0:T(8,128)(2,1)S(1)}, u32[]{:S(2)}, u32[]{:S(2)}) collective-permute-start(bf16[192,640]{1,0:T(8,128)(2,1)S(1)} %get-tuple-element.46), channel_id=1, source_target_pairs={{0,256},{256,512},{512,768},{768,0},{1,257},{257,513},{513,769},{7... | collective-permute-start | bytes 737288 | tf_op jit(solution)/shard_map/ppermute | solution.py:23
  57.0 5.5 %collective-permute-start.9 = (bf16[192,640]{1,0:T(8,128)(2,1)S(1)}, bf16[192,640]{1,0:T(8,128)(2,1)S(1)}, u32[]{:S(2)}, u32[]{:S(2)}) collective-permute-start(bf16[192,640]{1,0:T(8,128)(2,1)S(1)} %get-tuple-element.45), channel_id=1, source_target_pairs={{0,768},{256,0},{512,256},{768,512},{1,769},{257,1},{513,257},{769... | collective-permute-start | bytes 737288 | tf_op jit(solution)/shard_map/ppermute | solution.py:23
  62.5 1.9 %collective-permute-start.6 = (bf16[192,640]{1,0:T(8,128)(2,1)S(1)}, bf16[192,640]{1,0:T(8,128)(2,1)S(1)}, u32[]{:S(2)}, u32[]{:S(2)}) collective-permute-start(bf16[192,640]{1,0:T(8,128)(2,1)S(1)} %get-tuple-element.41), channel_id=1, source_target_pairs={{0,192},{64,0},{128,64},{192,128},{1,193},{65,1},{129,65},{193,129... | collective-permute-start | bytes 737288 | tf_op jit(solution)/shard_map/ppermute | solution.py:23
  64.4 3.9 %collective-permute-start.7 = (bf16[192,640]{1,0:T(8,128)(2,1)S(1)}, bf16[192,640]{1,0:T(8,128)(2,1)S(1)}, u32[]{:S(2)}, u32[]{:S(2)}) collective-permute-start(bf16[192,640]{1,0:T(8,128)(2,1)S(1)} %get-tuple-element.42), channel_id=1, source_target_pairs={{0,64},{64,128},{128,192},{192,0},{1,65},{65,129},{129,193},{193,1... | collective-permute-start | bytes 737288 | tf_op jit(solution)/shard_map/ppermute | solution.py:23
  68.4 4.1 %collective-permute-done.11 = bf16[192,640]{1,0:T(8,128)(2,1)S(1)} collective-permute-done((bf16[192,640]{1,0:T(8,128)(2,1)S(1)}, bf16[192,640]{1,0:T(8,128)(2,1)S(1)}, u32[]{:S(2)}, u32[]{:S(2)}) %collective-permute-start.11) | collective-permute-done | bytes 245792 | tf_op jit(solution)/shard_map/ppermute | solution.py:23
  72.5 1.9 %collective-permute-start.8 = (bf16[192,640]{1,0:T(8,128)(2,1)S(1)}, bf16[192,640]{1,0:T(8,128)(2,1)S(1)}, u32[]{:S(2)}, u32[]{:S(2)}) collective-permute-start(bf16[192,640]{1,0:T(8,128)(2,1)S(1)} %get-tuple-element.43), channel_id=1, source_target_pairs={{0,128},{64,192},{128,0},{192,64},{1,129},{65,193},{129,1},{193,65... | collective-permute-start | bytes 737288 | tf_op jit(solution)/shard_map/ppermute | solution.py:23
  74.4 0.9 %convert_add_fusion = f32[192,640]{1,0:T(8,128)} fusion(bf16[192,640]{1,0:T(8,128)(2,1)S(1)} %collective-permute-done.11, bf16[192,640]{1,0:T(8,128)(2,1)S(1)} %collective-permute-done.10, f32[192,640]{1,0:T(8,128)S(1)} %get-tuple-element.44, bf16[192,640]{1,0:T(8,128)(2,1)S(1)} %collective-permute-done.9), kind=kLoop, calls=%fused_computation | loop fusion | flops 737280 | bytes 1720320 | tf_op jit(solution)/shard_map/add | solution.py:136
  75.3 6.8 %collective-permute-done.8 = bf16[192,640]{1,0:T(8,128)(2,1)S(1)} collective-permute-done((bf16[192,640]{1,0:T(8,128)(2,1)S(1)}, bf16[192,640]{1,0:T(8,128)(2,1)S(1)}, u32[]{:S(2)}, u32[]{:S(2)}) %collective-permute-start.8) | collective-permute-done | bytes 245792 | tf_op jit(solution)/shard_map/ppermute | solution.py:23
  82.1 0.9 %convert_add_fusion.1 = f32[192,640]{1,0:T(8,128)} fusion(bf16[192,640]{1,0:T(8,128)(2,1)S(1)} %collective-permute-done.8, bf16[192,640]{1,0:T(8,128)(2,1)S(1)} %collective-permute-done.7, f32[192,640]{1,0:T(8,128)S(1)} %get-tuple-element.40, bf16[192,640]{1,0:T(8,128)(2,1)S(1)} %collective-permute-done.6), kind=kLoop, calls=%fused_computation.1 | loop fusion | flops 737280 | bytes 1720320 | tf_op jit(solution)/shard_map/add | solution.py:137
  (13 shorter events, 0.3 us)
Async XLA Ops:
  0.6 31.5 %collective-permute-start.4 = (bf16[192,640]{1,0:T(8,128)(2,1)}, bf16[192,640]{1,0:T(8,128)(2,1)S(1)}, u32[]{:S(2)}, u32[]{:S(2)}) collective-permute-start(bf16[192,640]{1,0:T(8,128)(2,1)} %t0.1), channel_id=1, source_target_pairs={{0,256},{256,512},{512,768},{768,0},{1,257},{257,513},{513,769},{7... | collective-permute-start | bytes 737288 | tf_op jit(solution)/shard_map/ppermute | solution.py:23
  7.1 31.3 %collective-permute-start.1 = (bf16[208,640]{1,0:T(8,128)(2,1)S(1)}, bf16[208,640]{1,0:T(8,128)(2,1)S(1)}, u32[]{:S(2)}, u32[]{:S(2)}) collective-permute-start(bf16[208,640]{1,0:T(8,128)(2,1)S(1)} %pad_maximum_fusion.i0), channel_id=1, source_target_pairs={{0,64},{64,128},{128,192},{192,0},{1,65},{65,129},{129,193},{193,1... | collective-permute-start | bytes 798728 | tf_op jit(solution)/shard_map/ppermute | solution.py:23
  10.2 28.2 %collective-permute-start.2 = (bf16[208,640]{1,0:T(8,128)(2,1)S(1)}, bf16[208,640]{1,0:T(8,128)(2,1)S(1)}, u32[]{:S(2)}, u32[]{:S(2)}) collective-permute-start(bf16[208,640]{1,0:T(8,128)(2,1)S(1)} %pad_maximum_fusion.i0), channel_id=1, source_target_pairs={{0,128},{64,192},{128,0},{192,64},{1,129},{65,193},{129,1},{193,65... | collective-permute-start | bytes 798728 | tf_op jit(solution)/shard_map/ppermute | solution.py:23
  21.5 16.9 %collective-permute-start.3 = (bf16[208,640]{1,0:T(8,128)(2,1)S(1)}, bf16[208,640]{1,0:T(8,128)(2,1)S(1)}, u32[]{:S(2)}, u32[]{:S(2)}) collective-permute-start(bf16[208,640]{1,0:T(8,128)(2,1)S(1)} %pad_maximum_fusion.i0), channel_id=1, source_target_pairs={{0,192},{64,0},{128,64},{192,128},{1,193},{65,1},{129,65},{193,129... | collective-permute-start | bytes 798728 | tf_op jit(solution)/shard_map/ppermute | solution.py:23
  26.0 12.4 %collective-permute-start.5 = (bf16[192,640]{1,0:T(8,128)(2,1)}, bf16[192,640]{1,0:T(8,128)(2,1)S(1)}, u32[]{:S(2)}, u32[]{:S(2)}) collective-permute-start(bf16[192,640]{1,0:T(8,128)(2,1)} %t0.1), channel_id=1, source_target_pairs={{0,768},{256,0},{512,256},{768,512},{1,769},{257,1},{513,257},{769... | collective-permute-start | bytes 737288 | tf_op jit(solution)/shard_map/ppermute | solution.py:23
  32.1 14.8 %collective-permute-start = (bf16[192,640]{1,0:T(8,128)(2,1)}, bf16[192,640]{1,0:T(8,128)(2,1)S(1)}, u32[]{:S(2)}, u32[]{:S(2)}) collective-permute-start(bf16[192,640]{1,0:T(8,128)(2,1)} %t0.1), channel_id=1, source_target_pairs={{0,512},{256,768},{512,0},{768,256},{1,513},{257,769},{513,1},{769... | collective-permute-start | bytes 737288 | tf_op jit(solution)/shard_map/ppermute | solution.py:23
  38.4 0.9 %copy-start = (bf16[192,640]{1,0:T(8,128)(2,1)S(1)}, bf16[192,640]{1,0:T(8,128)(2,1)}, u32[]{:S(2)}) copy-start(bf16[192,640]{1,0:T(8,128)(2,1)} %t0.1) | copy-start | bytes 737284
  48.8 23.7 %collective-permute-start.11 = (bf16[192,640]{1,0:T(8,128)(2,1)S(1)}, bf16[192,640]{1,0:T(8,128)(2,1)S(1)}, u32[]{:S(2)}, u32[]{:S(2)}) collective-permute-start(bf16[192,640]{1,0:T(8,128)(2,1)S(1)} %get-tuple-element.47), channel_id=1, source_target_pairs={{0,512},{256,768},{512,0},{768,256},{1,513},{257,769},{513,1},{769... | collective-permute-start | bytes 737288 | tf_op jit(solution)/shard_map/ppermute | solution.py:23
  50.8 23.6 %collective-permute-start.10 = (bf16[192,640]{1,0:T(8,128)(2,1)S(1)}, bf16[192,640]{1,0:T(8,128)(2,1)S(1)}, u32[]{:S(2)}, u32[]{:S(2)}) collective-permute-start(bf16[192,640]{1,0:T(8,128)(2,1)S(1)} %get-tuple-element.46), channel_id=1, source_target_pairs={{0,256},{256,512},{512,768},{768,0},{1,257},{257,513},{513,769},{7... | collective-permute-start | bytes 737288 | tf_op jit(solution)/shard_map/ppermute | solution.py:23
  57.0 17.4 %collective-permute-start.9 = (bf16[192,640]{1,0:T(8,128)(2,1)S(1)}, bf16[192,640]{1,0:T(8,128)(2,1)S(1)}, u32[]{:S(2)}, u32[]{:S(2)}) collective-permute-start(bf16[192,640]{1,0:T(8,128)(2,1)S(1)} %get-tuple-element.45), channel_id=1, source_target_pairs={{0,768},{256,0},{512,256},{768,512},{1,769},{257,1},{513,257},{769... | collective-permute-start | bytes 737288 | tf_op jit(solution)/shard_map/ppermute | solution.py:23
  62.5 12.8 %collective-permute-start.6 = (bf16[192,640]{1,0:T(8,128)(2,1)S(1)}, bf16[192,640]{1,0:T(8,128)(2,1)S(1)}, u32[]{:S(2)}, u32[]{:S(2)}) collective-permute-start(bf16[192,640]{1,0:T(8,128)(2,1)S(1)} %get-tuple-element.41), channel_id=1, source_target_pairs={{0,192},{64,0},{128,64},{192,128},{1,193},{65,1},{129,65},{193,129... | collective-permute-start | bytes 737288 | tf_op jit(solution)/shard_map/ppermute | solution.py:23
  64.4 10.9 %collective-permute-start.7 = (bf16[192,640]{1,0:T(8,128)(2,1)S(1)}, bf16[192,640]{1,0:T(8,128)(2,1)S(1)}, u32[]{:S(2)}, u32[]{:S(2)}) collective-permute-start(bf16[192,640]{1,0:T(8,128)(2,1)S(1)} %get-tuple-element.42), channel_id=1, source_target_pairs={{0,64},{64,128},{128,192},{192,0},{1,65},{65,129},{129,193},{193,1... | collective-permute-start | bytes 737288 | tf_op jit(solution)/shard_map/ppermute | solution.py:23
  72.5 9.6 %collective-permute-start.8 = (bf16[192,640]{1,0:T(8,128)(2,1)S(1)}, bf16[192,640]{1,0:T(8,128)(2,1)S(1)}, u32[]{:S(2)}, u32[]{:S(2)}) collective-permute-start(bf16[192,640]{1,0:T(8,128)(2,1)S(1)} %get-tuple-element.43), channel_id=1, source_target_pairs={{0,128},{64,192},{128,0},{192,64},{1,129},{65,193},{129,1},{193,65... | collective-permute-start | bytes 737288 | tf_op jit(solution)/shard_map/ppermute | solution.py:23

commit v2 on v0

v2 whole, which is shorter than its diff:
```python
import functools

import jax
import jax.numpy as jnp
from jax import lax
from jax.experimental import pallas as pl
from jax.experimental.pallas import tpu as pltpu
from jax.sharding import Mesh, PartitionSpec as P

logit_scale = 25.0
logit_bias = -1.0
sides = 4
send_type = jnp.bfloat16
label_base = 64
pad_rows = 16

nt = (((1,), (1,)), ((), ()))
tn = (((0,), (0,)), ((), ()))
vmem = pl.BlockSpec(memory_space=pltpu.VMEM)
params = pltpu.CompilerParams(vmem_limit_bytes=48 * 1024 * 1024)


def shifted(value, axis, steps):
    pairs = [(source, (source + steps) % sides) for source in range(sides)]
    return lax.ppermute(value, axis, pairs)


def together(*values):
    return lax.optimization_barrier(values)


def bundle_kernel(images, labels, out):
    rows, width = images.shape
    out[:rows, :] = images[...]
    value = labels[...]
    high = value // label_base
    low = value - high * label_base
    line = lax.broadcasted_iota(jnp.int32, (pad_rows, rows), 0)
    digits = jnp.where(line == 0, high, jnp.where(line == 1, low, 0))
    out[rows:, :rows] = digits.astype(jnp.float32).astype(jnp.bfloat16)
    out[rows:, rows:] = jnp.zeros((pad_rows, width - rows), jnp.bfloat16)


def coefficients(text_rows, images, labels, text_ids):
    logits = (
        logit_scale
        * lax.dot_general(text_rows, images, nt, preferred_element_type=jnp.float32)
        + logit_bias
    )
    paired = labels == text_ids
    small = 1.0 / (1.0 + jnp.exp(jnp.where(paired, logits, -logits)))
    return jnp.where(paired, -small, small).astype(jnp.bfloat16)


def text_kernel(scale, bundles, t0, t2, t1, t3, own, up, far, down, images, coeff, labs):
    rows = t0.shape[0]
    for k in range(sides):
        images[k * rows : (k + 1) * rows, :] = bundles[k, :rows, :]
        digits = bundles[k, rows:, :].astype(jnp.float32)
        labs[k : k + 1, :] = label_base * digits[0:1, :rows] + digits[1:2, :rows]
    labels = jnp.concatenate([labs[k : k + 1, :] for k in range(sides)], axis=1)
    y, x = lax.axis_index("yh"), lax.axis_index("xx")
    line = lax.broadcasted_iota(jnp.int32, (rows, 1), 0)
    for n, (texts, out) in enumerate(((t0, own), (t1, up), (t2, far), (t3, down))):
        first = (lax.rem(y + (sides - n), sides) * sides + x) * rows
        ids = (first + line).astype(jnp.float32)
        c = coefficients(texts[...], images[...], labels, ids)
        coeff[n * rows : (n + 1) * rows, :] = c
        out[...] = (scale * jnp.dot(c, images[...], preferred_element_type=jnp.float32)).astype(out.dtype)


def image_kernel(scale, coeff, t0, t1, t2, t3, g0, g1, g2, g3, total):
    rows = t0.shape[0]
    value = None
    for n, texts in enumerate((t0, t1, t2, t3)):
        term = lax.dot_general(coeff[n * rows : (n + 1) * rows, :], texts[...], tn, preferred_element_type=jnp.float32)
        value = term if value is None else value + term
    for k in range(sides):
        total[k] = scale * value[k * rows : (k + 1) * rows, :]
    x = lax.axis_index("xx")
    for k, out in enumerate((g0, g1, g2, g3)):
        out[...] = total[lax.rem(x + (sides - k), sides)].astype(out.dtype)


def sum_kernel(h0, y1, y2, y3, g0, x1, x2, x3, image_grads, text_grads):
    f32 = jnp.float32
    image_grads[...] = g0[...] + x1[...].astype(f32) + x2[...].astype(f32) + x3[...].astype(f32)
    text_grads[...] = h0[...] + y1[...].astype(f32) + y2[...].astype(f32) + y3[...].astype(f32)


def call(kernel, inputs, shapes, scratch=(), flops=0):
    return pl.pallas_call(
        kernel,
        out_shape=shapes,
        in_specs=[vmem] * inputs,
        out_specs=[vmem] * len(shapes),
        scratch_shapes=list(scratch),
        compiler_params=params,
        cost_estimate=pl.CostEstimate(flops=flops, bytes_accessed=4 << 20, transcendentals=0),
    )


def on_device(image_embeddings, text_embeddings, pair_labels):
    rows, width = text_embeddings.shape
    scale = logit_scale / (sides * sides)
    f32 = jnp.float32
    block = (rows, width)
    every = sides * rows

    (bundle,) = call(bundle_kernel, 2, [jax.ShapeDtypeStruct((rows + pad_rows, width), jnp.bfloat16)])(
        image_embeddings, pair_labels.reshape(1, rows)
    )
    texts = text_embeddings
    text_2 = shifted(texts, "yh", 2)
    text_3 = shifted(texts, "yh", -1)
    text_1 = shifted(texts, "yh", 1)
    bundles = lax.all_gather(bundle, "xx", axis=0)

    own, up, far, down, images, coeff = call(
        functools.partial(text_kernel, scale),
        5,
        [
            jax.ShapeDtypeStruct(block, f32),
            jax.ShapeDtypeStruct(block, send_type),
            jax.ShapeDtypeStruct(block, send_type),
            jax.ShapeDtypeStruct(block, send_type),
            jax.ShapeDtypeStruct((every, width), jnp.bfloat16),
            jax.ShapeDtypeStruct((every, every), jnp.bfloat16),
        ],
        [pltpu.VMEM((8, rows), f32)],
        4 * every * every * width,
    )(bundles, texts, text_2, text_1, text_3)
    back_2 = shifted(far, "yh", 2)
    back_1 = shifted(up, "yh", -1)
    back_3 = shifted(down, "yh", 1)
    g0, g1, g2, g3 = call(
        functools.partial(image_kernel, scale),
        5,
        [jax.ShapeDtypeStruct(block, f32)] + [jax.ShapeDtypeStruct(block, send_type)] * 3,
        [pltpu.VMEM((sides,) + block, f32)],
        2 * every * every * width,
    )(coeff, texts, text_1, text_2, text_3)
    grad_1 = shifted(g1, "xx", -1)
    grad_2 = shifted(g2, "xx", 2)
    grad_3 = shifted(g3, "xx", 1)
    image_grads, text_grads = call(sum_kernel, 8, [jax.ShapeDtypeStruct(block, f32)] * 2)(
        own, back_2, back_1, back_3, g0, grad_2, grad_1, grad_3
    )
    return image_grads, text_grads


def solution(mesh):
    grid = Mesh(mesh.devices.reshape(sides, sides, -1), ("yh", "xx", "dp"))
    rows = P(("dp", "yh", "xx"), None)
    return jax.shard_map(
        on_device,
        mesh=grid,
        in_specs=(rows, rows, P(("dp", "yh", "xx"))),
        out_specs=(rows, rows),
        check_vma=False,
    )
```

time: 642 us -> 99.3 us (0.15)
  the two profiles are of different devices: /device:TPU:264 before, /device:TPU:16 now
where the time goes in v2:
time: 99.3 us; the launch traced here: 98.7 us
  starting transfers between devices  45.7 us (46%)
  waiting for transfers between devices  28 us (28%)
  between operations  14.1 us (14%)
  Pallas kernels  7.1 us (7%)
  local copies, waits for them, and re-layouts  3.79 us (4%)
    ppermute x9, starting transfers between devices, shifted(): return lax.ppermute(value, axis, pairs)  45.6 us
    ppermute x9, waiting for transfers between devices, shifted(): return lax.ppermute(value, axis, pairs)  15.5 us
    all_gather x1, waiting for transfers between devices, on_device(): bundles = lax.all_gather(bundle, 'xx', axis=0)  12.5 us
    unnamed x10, local copies, waits for them, and re-layouts  3.79 us
    pallas_call x1, Pallas kernels, on_device(): call(functools.partial(text_kernel, scale), 5, [jax.ShapeDtypeStruct(bloc...  3.6 us
  transfers between devices with their start and end apart: 10, of which 6 were waited for; matrix products, arithmetic and copies ran while one was open for 0% of the time, Pallas kernels for 2%

profile of v2, /device:TPU:16, one launch (start us, length us, event | category | flops | bytes accessed | tf_op | source)
XLA Modules:
  0.0 98.7 jit_solution(7466417243668204329)
XLA Ops:
  7.2 0.0 all-gather.3.cloned.1.call-start
  7.2 0.9 copy-done
  8.2 0.7 copy-done.1
  8.8 0.7 shard_map.50
  9.6 14.9 %collective-permute-start.2 = (bf16[192,640]{1,0:T(8,128)(2,1)}, bf16[192,640]{1,0:T(8,128)(2,1)S(1)}, u32[]{:S(2)}, u32[]{:S(2)}) collective-permute-start(bf16[192,640]{1,0:T(8,128)(2,1)} %t0.3), channel_id=1, source_target_pairs={{0,768},{256,0},{512,256},{768,512},{1,769},{257,1},{513,257},{769... | collective-permute-start | bytes 737288 | tf_op jit(solution)/shard_map/ppermute | solution.py:25
  24.5 1.9 %collective-permute-start.1 = (bf16[192,640]{1,0:T(8,128)(2,1)}, bf16[192,640]{1,0:T(8,128)(2,1)S(1)}, u32[]{:S(2)}, u32[]{:S(2)}) collective-permute-start(bf16[192,640]{1,0:T(8,128)(2,1)} %t0.3), channel_id=1, source_target_pairs={{0,256},{256,512},{512,768},{768,0},{1,257},{257,513},{513,769},{7... | collective-permute-start | bytes 737288 | tf_op jit(solution)/shard_map/ppermute | solution.py:25
  26.4 5.5 %collective-permute-start = (bf16[192,640]{1,0:T(8,128)(2,1)}, bf16[192,640]{1,0:T(8,128)(2,1)S(1)}, u32[]{:S(2)}, u32[]{:S(2)}) collective-permute-start(bf16[192,640]{1,0:T(8,128)(2,1)} %t0.3), channel_id=1, source_target_pairs={{0,512},{256,768},{512,0},{768,256},{1,513},{257,769},{513,1},{769... | collective-permute-start | bytes 737288 | tf_op jit(solution)/shard_map/ppermute | solution.py:25
  31.9 5.9 %collective-permute-done.2.t3 = bf16[192,640]{1,0:T(8,128)(2,1)S(1)} collective-permute-done((bf16[192,640]{1,0:T(8,128)(2,1)}, bf16[192,640]{1,0:T(8,128)(2,1)S(1)}, u32[]{:S(2)}, u32[]{:S(2)}) %collective-permute-start.2) | collective-permute-done | bytes 245792 | tf_op jit(solution)/shard_map/ppermute | solution.py:25
  37.8 3.3 %collective-permute-done.t2 = bf16[192,640]{1,0:T(8,128)(2,1)S(1)} collective-permute-done((bf16[192,640]{1,0:T(8,128)(2,1)}, bf16[192,640]{1,0:T(8,128)(2,1)S(1)}, u32[]{:S(2)}, u32[]{:S(2)}) %collective-permute-start) | collective-permute-done | bytes 245792 | tf_op jit(solution)/shard_map/ppermute | solution.py:25
  41.1 12.5 %all-gather.3.cloned.1.call-done = bf16[832,640]{1,0:T(8,128)(2,1)} async-done(((bf16[208,640]{1,0:T(8,128)(2,1)}), bf16[832,640]{1,0:T(8,128)(2,1)}) %all-gather.3.cloned.1.call-update) | async-done | bytes 1064976 | tf_op jit(solution)/shard_map/all_gather | solution.py:117
  53.5 1.2 %copy-done.2 = bf16[832,640]{1,0:T(8,128)(2,1)S(1)} copy-done((bf16[832,640]{1,0:T(8,128)(2,1)S(1)}, bf16[832,640]{1,0:T(8,128)(2,1)}, u32[]{:S(2)}) %copy-start.2) | copy-done | bytes 1064984
  54.8 0.9 copy-done.3
  55.7 3.6 %shard_map.51 = (f32[192,640]{1,0:T(8,128)S(1)}, bf16[192,640]{1,0:T(8,128)(2,1)S(1)}, bf16[192,640]{1,0:T(8,128)(2,1)S(1)}, bf16[192,640]{1,0:T(8,128)(2,1)S(1)...) custom-call(bf16[4,208,640]{2,1,0:T(8,128)(2,1)S(1)} %bitcast.3, bf16[192,640]{1,0:T(8,128)(2,1)S(1)} %copy-done.3, ...), custom_call_target="tpu_custom_call" | custom-call | flops 1509949440 | bytes 4194304 | tf_op jit(solution)/shard_map/pallas_call | solution.py:119
  59.3 5.6 %collective-permute-start.3 = (bf16[192,640]{1,0:T(8,128)(2,1)S(1)}, bf16[192,640]{1,0:T(8,128)(2,1)S(1)}, u32[]{:S(2)}, u32[]{:S(2)}) collective-permute-start(bf16[192,640]{1,0:T(8,128)(2,1)S(1)} %get-tuple-element.12), channel_id=1, source_target_pairs={{0,512},{256,768},{512,0},{768,256},{1,513},{257,769},{513,1},{769... | collective-permute-start | bytes 737288 | tf_op jit(solution)/shard_map/ppermute | solution.py:25
  64.9 4.2 %collective-permute-start.4 = (bf16[192,640]{1,0:T(8,128)(2,1)S(1)}, bf16[192,640]{1,0:T(8,128)(2,1)S(1)}, u32[]{:S(2)}, u32[]{:S(2)}) collective-permute-start(bf16[192,640]{1,0:T(8,128)(2,1)S(1)} %get-tuple-element.13), channel_id=1, source_target_pairs={{0,768},{256,0},{512,256},{768,512},{1,769},{257,1},{513,257},{769... | collective-permute-start | bytes 737288 | tf_op jit(solution)/shard_map/ppermute | solution.py:25
  69.1 3.7 %collective-permute-start.5 = (bf16[192,640]{1,0:T(8,128)(2,1)S(1)}, bf16[192,640]{1,0:T(8,128)(2,1)S(1)}, u32[]{:S(2)}, u32[]{:S(2)}) collective-permute-start(bf16[192,640]{1,0:T(8,128)(2,1)S(1)} %get-tuple-element.14), channel_id=1, source_target_pairs={{0,256},{256,512},{512,768},{768,0},{1,257},{257,513},{513,769},{7... | collective-permute-start | bytes 737288 | tf_op jit(solution)/shard_map/ppermute | solution.py:25
  72.9 1.7 %shard_map.52 = (f32[192,640]{1,0:T(8,128)S(1)}, bf16[192,640]{1,0:T(8,128)(2,1)S(1)}, bf16[192,640]{1,0:T(8,128)(2,1)S(1)}, bf16[192,640]{1,0:T(8,128)(2,1)S(1)}) custom-call(bf16[768,768]{1,0:T(8,128)(2,1)S(1)} %get-tuple-element.15.coeff, bf16[192,640]{1,0:T(8,128)(2,1)S(1)} %copy-done.4, bf16[192,640]{1,0:T(8,128)(2,1)S(1)} %collective-permute-done.1.t1, ...), custom_call_target="tpu_custom_call" | custom-call | flops 754974720 | bytes 4194304 | tf_op jit(solution)/shard_map/pallas_call | solution.py:136
  74.6 4.0 %collective-permute-start.6 = (bf16[192,640]{1,0:T(8,128)(2,1)S(1)}, bf16[192,640]{1,0:T(8,128)(2,1)S(1)}, u32[]{:S(2)}, u32[]{:S(2)}) collective-permute-start(bf16[192,640]{1,0:T(8,128)(2,1)S(1)} %get-tuple-element.17), channel_id=1, source_target_pairs={{0,128},{64,192},{128,0},{192,64},{1,129},{65,193},{129,1},{193,65... | collective-permute-start | bytes 737288 | tf_op jit(solution)/shard_map/ppermute | solution.py:25
  78.6 2.9 %collective-permute-start.7 = (bf16[192,640]{1,0:T(8,128)(2,1)S(1)}, bf16[192,640]{1,0:T(8,128)(2,1)S(1)}, u32[]{:S(2)}, u32[]{:S(2)}) collective-permute-start(bf16[192,640]{1,0:T(8,128)(2,1)S(1)} %get-tuple-element.18), channel_id=1, source_target_pairs={{0,192},{64,0},{128,64},{192,128},{1,193},{65,1},{129,65},{193,129... | collective-permute-start | bytes 737288 | tf_op jit(solution)/shard_map/ppermute | solution.py:25
  81.5 2.9 %collective-permute-start.8 = (bf16[192,640]{1,0:T(8,128)(2,1)S(1)}, bf16[192,640]{1,0:T(8,128)(2,1)S(1)}, u32[]{:S(2)}, u32[]{:S(2)}) collective-permute-start(bf16[192,640]{1,0:T(8,128)(2,1)S(1)} %get-tuple-element.19), channel_id=1, source_target_pairs={{0,64},{64,128},{128,192},{192,0},{1,65},{65,129},{129,193},{193,1... | collective-permute-start | bytes 737288 | tf_op jit(solution)/shard_map/ppermute | solution.py:25
  84.5 2.4 %collective-permute-done.4.y2 = bf16[192,640]{1,0:T(8,128)(2,1)S(1)} collective-permute-done((bf16[192,640]{1,0:T(8,128)(2,1)S(1)}, bf16[192,640]{1,0:T(8,128)(2,1)S(1)}, u32[]{:S(2)}, u32[]{:S(2)}) %collective-permute-start.4) | collective-permute-done | bytes 245792 | tf_op jit(solution)/shard_map/ppermute | solution.py:25
  86.9 1.5 %collective-permute-done.7.x2 = bf16[192,640]{1,0:T(8,128)(2,1)S(1)} collective-permute-done((bf16[192,640]{1,0:T(8,128)(2,1)S(1)}, bf16[192,640]{1,0:T(8,128)(2,1)S(1)}, u32[]{:S(2)}, u32[]{:S(2)}) %collective-permute-start.7) | collective-permute-done | bytes 245792 | tf_op jit(solution)/shard_map/ppermute | solution.py:25
  88.4 2.4 %collective-permute-done.8.x3 = bf16[192,640]{1,0:T(8,128)(2,1)S(1)} collective-permute-done((bf16[192,640]{1,0:T(8,128)(2,1)S(1)}, bf16[192,640]{1,0:T(8,128)(2,1)S(1)}, u32[]{:S(2)}, u32[]{:S(2)}) %collective-permute-start.8) | collective-permute-done | bytes 245792 | tf_op jit(solution)/shard_map/ppermute | solution.py:25
  90.8 1.1 %shard_map.53 = (f32[192,640]{1,0:T(8,128)}, f32[192,640]{1,0:T(8,128)}) custom-call(f32[192,640]{1,0:T(8,128)S(1)} %get-tuple-element.11.h0, bf16[192,640]{1,0:T(8,128)(2,1)S(1)} %collective-permute-done.3.y1, bf16[192,640]{1,0:T(8,128)(2,1)S(1)} %collective-permute-done.4.y2, bf16[192,640]{1,0:T(8,128)(2,1)S(1)} %collective-permute-done.5.y3, ...), custom_call_target="tpu_custom_call" | custom-call | bytes 4194304 | tf_op jit(solution)/shard_map/pallas_call | solution.py:146
  (11 shorter events, 0.0 us)
Async XLA Ops:
  7.2 46.4 %all-gather.3.cloned.1.call-start = ((), (), s32[]{:S(2)}) async-start(), calls=%async_computation | async-start | bytes 1331200 | tf_op jit(solution)/shard_map/all_gather | solution.py:117
  7.2 0.9 copy-start
  8.2 0.7 copy-start.1
  9.6 28.2 %collective-permute-start.2 = (bf16[192,640]{1,0:T(8,128)(2,1)}, bf16[192,640]{1,0:T(8,128)(2,1)S(1)}, u32[]{:S(2)}, u32[]{:S(2)}) collective-permute-start(bf16[192,640]{1,0:T(8,128)(2,1)} %t0.3), channel_id=1, source_target_pairs={{0,768},{256,0},{512,256},{768,512},{1,769},{257,1},{513,257},{769... | collective-permute-start | bytes 737288 | tf_op jit(solution)/shard_map/ppermute | solution.py:25
  24.5 13.3 %collective-permute-start.1 = (bf16[192,640]{1,0:T(8,128)(2,1)}, bf16[192,640]{1,0:T(8,128)(2,1)S(1)}, u32[]{:S(2)}, u32[]{:S(2)}) collective-permute-start(bf16[192,640]{1,0:T(8,128)(2,1)} %t0.3), channel_id=1, source_target_pairs={{0,256},{256,512},{512,768},{768,0},{1,257},{257,513},{513,769},{7... | collective-permute-start | bytes 737288 | tf_op jit(solution)/shard_map/ppermute | solution.py:25
  26.4 14.7 %collective-permute-start = (bf16[192,640]{1,0:T(8,128)(2,1)}, bf16[192,640]{1,0:T(8,128)(2,1)S(1)}, u32[]{:S(2)}, u32[]{:S(2)}) collective-permute-start(bf16[192,640]{1,0:T(8,128)(2,1)} %t0.3), channel_id=1, source_target_pairs={{0,512},{256,768},{512,0},{768,256},{1,513},{257,769},{513,1},{769... | collective-permute-start | bytes 737288 | tf_op jit(solution)/shard_map/ppermute | solution.py:25
  53.5 1.2 %copy-start.2 = (bf16[832,640]{1,0:T(8,128)(2,1)S(1)}, bf16[832,640]{1,0:T(8,128)(2,1)}, u32[]{:S(2)}) copy-start(bf16[832,640]{1,0:T(8,128)(2,1)} %all-gather.3.cloned.1.call-done) | copy-start | bytes 3194884
  54.8 0.9 copy-start.3
  55.7 17.1 %copy-start.4 = (bf16[192,640]{1,0:T(8,128)(2,1)S(1)}, bf16[192,640]{1,0:T(8,128)(2,1)}, u32[]{:S(2)}) copy-start(bf16[192,640]{1,0:T(8,128)(2,1)} %t0.3) | copy-start | bytes 737284
  59.3 22.2 %collective-permute-start.3 = (bf16[192,640]{1,0:T(8,128)(2,1)S(1)}, bf16[192,640]{1,0:T(8,128)(2,1)S(1)}, u32[]{:S(2)}, u32[]{:S(2)}) collective-permute-start(bf16[192,640]{1,0:T(8,128)(2,1)S(1)} %get-tuple-element.12), channel_id=1, source_target_pairs={{0,512},{256,768},{512,0},{768,256},{1,513},{257,769},{513,1},{769... | collective-permute-start | bytes 737288 | tf_op jit(solution)/shard_map/ppermute | solution.py:25
  64.9 22.0 %collective-permute-start.4 = (bf16[192,640]{1,0:T(8,128)(2,1)S(1)}, bf16[192,640]{1,0:T(8,128)(2,1)S(1)}, u32[]{:S(2)}, u32[]{:S(2)}) collective-permute-start(bf16[192,640]{1,0:T(8,128)(2,1)S(1)} %get-tuple-element.13), channel_id=1, source_target_pairs={{0,768},{256,0},{512,256},{768,512},{1,769},{257,1},{513,257},{769... | collective-permute-start | bytes 737288 | tf_op jit(solution)/shard_map/ppermute | solution.py:25
  69.1 17.8 %collective-permute-start.5 = (bf16[192,640]{1,0:T(8,128)(2,1)S(1)}, bf16[192,640]{1,0:T(8,128)(2,1)S(1)}, u32[]{:S(2)}, u32[]{:S(2)}) collective-permute-start(bf16[192,640]{1,0:T(8,128)(2,1)S(1)} %get-tuple-element.14), channel_id=1, source_target_pairs={{0,256},{256,512},{512,768},{768,0},{1,257},{257,513},{513,769},{7... | collective-permute-start | bytes 737288 | tf_op jit(solution)/shard_map/ppermute | solution.py:25
  74.6 12.3 %collective-permute-start.6 = (bf16[192,640]{1,0:T(8,128)(2,1)S(1)}, bf16[192,640]{1,0:T(8,128)(2,1)S(1)}, u32[]{:S(2)}, u32[]{:S(2)}) collective-permute-start(bf16[192,640]{1,0:T(8,128)(2,1)S(1)} %get-tuple-element.17), channel_id=1, source_target_pairs={{0,128},{64,192},{128,0},{192,64},{1,129},{65,193},{129,1},{193,65... | collective-permute-start | bytes 737288 | tf_op jit(solution)/shard_map/ppermute | solution.py:25
  78.6 9.8 %collective-permute-start.7 = (bf16[192,640]{1,0:T(8,128)(2,1)S(1)}, bf16[192,640]{1,0:T(8,128)(2,1)S(1)}, u32[]{:S(2)}, u32[]{:S(2)}) collective-permute-start(bf16[192,640]{1,0:T(8,128)(2,1)S(1)} %get-tuple-element.18), channel_id=1, source_target_pairs={{0,192},{64,0},{128,64},{192,128},{1,193},{65,1},{129,65},{193,129... | collective-permute-start | bytes 737288 | tf_op jit(solution)/shard_map/ppermute | solution.py:25
  81.5 9.3 %collective-permute-start.8 = (bf16[192,640]{1,0:T(8,128)(2,1)S(1)}, bf16[192,640]{1,0:T(8,128)(2,1)S(1)}, u32[]{:S(2)}, u32[]{:S(2)}) collective-permute-start(bf16[192,640]{1,0:T(8,128)(2,1)S(1)} %get-tuple-element.19), channel_id=1, source_target_pairs={{0,64},{64,128},{128,192},{192,0},{1,65},{65,129},{129,193},{193,1... | collective-permute-start | bytes 737288 | tf_op jit(solution)/shard_map/ppermute | solution.py:25
Sparse Core Ops, SparseCore 0:
  11.3 42.2 all-gather.2

commit v3 on v2

v3 whole, which is shorter than its diff:
```python
import functools

import jax
import jax.numpy as jnp
from jax import lax
from jax.experimental import pallas as pl
from jax.experimental.pallas import tpu as pltpu
from jax.sharding import Mesh, PartitionSpec as P

logit_scale = 25.0
logit_bias = -1.0
sides = 4
send_type = jnp.bfloat16
label_base = 64
pad_rows = 16

nt = (((1,), (1,)), ((), ()))
tn = (((0,), (0,)), ((), ()))
vmem = pl.BlockSpec(memory_space=pltpu.VMEM)
hbm = pl.BlockSpec(memory_space=pltpu.HBM)
params = pltpu.CompilerParams(vmem_limit_bytes=48 * 1024 * 1024)


def shifted(value, axis, steps):
    pairs = [(source, (source + steps) % sides) for source in range(sides)]
    return lax.ppermute(value, axis, pairs)


def together(*values):
    return lax.optimization_barrier(values)


def copies_kernel(texts, out, sems):
    moves = [pltpu.make_async_copy(texts, out.at[k], sems.at[k]) for k in range(sides)]
    for move in moves:
        move.start()
    for move in moves:
        move.wait()


def bundle_kernel(images, labels, out):
    rows, width = images.shape
    out[:rows, :] = images[...]
    value = labels[...]
    high = value // label_base
    low = value - high * label_base
    line = lax.broadcasted_iota(jnp.int32, (pad_rows, rows), 0)
    digits = jnp.where(line == 0, high, jnp.where(line == 1, low, 0))
    out[rows:, :rows] = digits.astype(jnp.float32).astype(jnp.bfloat16)
    out[rows:, rows:] = jnp.zeros((pad_rows, width - rows), jnp.bfloat16)


def coefficients(text_rows, images, labels, text_ids):
    logits = (
        logit_scale
        * lax.dot_general(text_rows, images, nt, preferred_element_type=jnp.float32)
        + logit_bias
    )
    paired = labels == text_ids
    small = 1.0 / (1.0 + jnp.exp(jnp.where(paired, logits, -logits)))
    return jnp.where(paired, -small, small).astype(jnp.bfloat16)


def text_ids(first, rows):
    line = lax.broadcasted_iota(jnp.int32, (rows, 1), 0)
    return (first * rows + line).astype(jnp.float32)


def near_kernel(scale, i0, i1, i2, i3, texts, own, images, labels, coeff, labs):
    rows = own.shape[0]
    for k, bundle in enumerate((i0, i1, i2, i3)):
        images[k * rows : (k + 1) * rows, :] = bundle[:rows, :]
        digits = bundle[rows:, :].astype(jnp.float32)
        labs[k : k + 1, :] = label_base * digits[0:1, :rows] + digits[1:2, :rows]
    labels[...] = jnp.concatenate([labs[k : k + 1, :] for k in range(sides)], axis=1)
    y, x = lax.axis_index("yh"), lax.axis_index("xx")
    c = coefficients(texts[...], images[...], labels[...], text_ids(y * sides + x, rows))
    coeff[...] = c
    own[...] = scale * jnp.dot(c, images[...], preferred_element_type=jnp.float32)


def far_kernel(scale, stack, images, labels, parts, coeff, made, sems):
    rows = stack.shape[1]
    y, x = lax.axis_index("yh"), lax.axis_index("xx")
    moves = []
    for n in range(sides - 1):
        owner = lax.rem(y + (n + 1), sides)
        c = coefficients(stack[owner], images[...], labels[...], text_ids(owner * sides + x, rows))
        coeff[n * rows : (n + 1) * rows, :] = c
        made[n] = (scale * jnp.dot(c, images[...], preferred_element_type=jnp.float32)).astype(made.dtype)
        moves.append(pltpu.make_async_copy(made.at[n], parts.at[owner], sems.at[n]))
        moves[-1].start()
    for move in moves:
        move.wait()


def image_kernel(scale, near, coeff, texts, stack, g0, g1, g2, g3):
    rows = g0.shape[0]
    y = lax.axis_index("yh")
    value = lax.dot_general(near[...], texts[...], tn, preferred_element_type=jnp.float32)
    for n in range(sides - 1):
        value = value + lax.dot_general(
            coeff[n * rows : (n + 1) * rows, :],
            stack[lax.rem(y + (n + 1), sides)],
            tn,
            preferred_element_type=jnp.float32,
        )
    for k, out in enumerate((g0, g1, g2, g3)):
        out[...] = (scale * value[k * rows : (k + 1) * rows, :]).astype(out.dtype)


def sum_kernel(own, parts, g0, x1, x2, x3, image_grads, text_grads):
    f32 = jnp.float32
    image_grads[...] = g0[...] + x1[...].astype(f32) + x2[...].astype(f32) + x3[...].astype(f32)
    y = lax.axis_index("yh")
    total = own[...]
    for step in range(1, sides):
        total = total + parts[lax.rem(y + step, sides)].astype(f32)
    text_grads[...] = total


def call(kernel, shapes, scratch=(), flops=0, outputs=None):
    def run(*operands):
        return pl.pallas_call(
            kernel,
            out_shape=shapes,
            in_specs=[vmem] * len(operands),
            out_specs=[vmem] * len(shapes) if outputs is None else outputs,
            scratch_shapes=list(scratch),
            compiler_params=params,
            cost_estimate=pl.CostEstimate(flops=flops, bytes_accessed=4 << 20, transcendentals=0),
        )(*operands)

    return run


def on_device(image_embeddings, text_embeddings, pair_labels):
    rows, width = text_embeddings.shape
    scale = logit_scale / (sides * sides)
    f32 = jnp.float32
    block = (rows, width)
    every = sides * rows

    dots = 2 * rows * every * width
    half = jnp.bfloat16
    shape = jax.ShapeDtypeStruct

    (copies,) = call(
        copies_kernel,
        [shape((sides,) + block, half)],
        [pltpu.SemaphoreType.DMA((sides,))],
        outputs=[hbm],
    )(text_embeddings)
    (bundle,) = call(bundle_kernel, [shape((rows + pad_rows, width), half)])(
        image_embeddings, pair_labels.reshape(1, rows)
    )
    stack = lax.all_to_all(copies, "yh", 0, 0)
    image_1 = shifted(bundle, "xx", 1)
    image_2 = shifted(bundle, "xx", 2)
    image_3 = shifted(bundle, "xx", -1)

    own, images, labels, near = call(
        functools.partial(near_kernel, scale),
        [shape(block, f32), shape((every, width), half), shape((1, every), f32), shape((rows, every), half)],
        [pltpu.VMEM((8, rows), f32)],
        2 * dots,
    )(bundle, image_1, image_2, image_3, text_embeddings)
    parts, coeff = call(
        functools.partial(far_kernel, scale),
        [shape((sides,) + block, send_type), shape(((sides - 1) * rows, every), half)],
        [pltpu.VMEM((sides - 1,) + block, send_type), pltpu.SemaphoreType.DMA((sides - 1,))],
        6 * dots,
        outputs=[hbm, vmem],
    )(stack, images, labels)
    parts = lax.all_to_all(parts, "yh", 0, 0)
    g0, g1, g2, g3 = call(
        functools.partial(image_kernel, scale),
        [shape(block, f32)] + [shape(block, send_type)] * 3,
        (),
        4 * dots,
    )(near, coeff, text_embeddings, stack)
    grad_1 = shifted(g1, "xx", -1)
    grad_2 = shifted(g2, "xx", 2)
    grad_3 = shifted(g3, "xx", 1)
    image_grads, text_grads = call(sum_kernel, [shape(block, f32)] * 2)(
        own, parts, g0, grad_1, grad_2, grad_3
    )
    return image_grads, text_grads


def solution(mesh):
    grid = Mesh(mesh.devices.reshape(sides, sides, -1), ("yh", "xx", "dp"))
    rows = P(("dp", "yh", "xx"), None)
    return jax.shard_map(
        on_device,
        mesh=grid,
        in_specs=(rows, rows, P(("dp", "yh", "xx"))),
        out_specs=(rows, rows),
        check_vma=False,
    )
```

time: 99.3 us -> 69.7 us (0.70)
  the two profiles are of different devices: /device:TPU:16 before, /device:TPU:466 now
where the time goes in v3:
time: 69.7 us; the launch traced here: 69.2 us
  starting transfers between devices  32.8 us (47%)
  waiting for transfers between devices  24.4 us (35%)
  Pallas kernels  7.51 us (11%)
  local copies, waits for them, and re-layouts  3.73 us (5%)
  between operations  0.75 us (1%)
    ppermute x6, starting transfers between devices, shifted(): return lax.ppermute(value, axis, pairs)  21.1 us
    ppermute x6, waiting for transfers between devices, shifted(): return lax.ppermute(value, axis, pairs)  16.6 us
    all_to_all x1, starting transfers between devices, on_device(): stack = lax.all_to_all(copies, 'yh', 0, 0)  7.57 us
    pallas_call x6, Pallas kernels, run(): pl.pallas_call(kernel, out_shape=shapes, in_specs=[vmem] * len(operands),...  7.51 us
    all_to_all x1, waiting for transfers between devices, on_device(): parts = lax.all_to_all(parts, 'yh', 0, 0)  4.38 us
    all_to_all x1, starting transfers between devices, on_device(): parts = lax.all_to_all(parts, 'yh', 0, 0)  4.19 us
    unnamed x12, local copies, waits for them, and re-layouts  3.73 us
    all_to_all x1, waiting for transfers between devices, on_device(): stack = lax.all_to_all(copies, 'yh', 0, 0)  3.38 us
  transfers between devices with their start and end apart: 8, of which 7 were waited for; matrix products, arithmetic and copies ran while one was open for 0% of the time, Pallas kernels for 3%

profile of v3, /device:TPU:466, one launch (start us, length us, event | category | flops | bytes accessed | tf_op | source)
XLA Modules:
  0.0 69.2 jit_solution(9987700894779477306)
XLA Ops:
  0.6 0.9 %copy-done = bf16[192,640]{1,0:T(8,128)(2,1)S(1)} copy-done((bf16[192,640]{1,0:T(8,128)(2,1)S(1)}, bf16[192,640]{1,0:T(8,128)(2,1)}, u32[]{:S(2)}) %copy-start) | copy-done | bytes 245784
  1.6 1.0 %shard_map.52 = bf16[4,192,640]{2,1,0:T(8,128)(2,1)} custom-call(bf16[192,640]{1,0:T(8,128)(2,1)S(1)} %copy-done), custom_call_target="tpu_custom_call" | custom-call | bytes 4194304 | tf_op jit(solution)/shard_map/pallas_call | solution.py:124
  2.6 7.6 %all-to-all-start = ((bf16[4,192,640]{2,1,0:T(8,128)(2,1)}), bf16[4,192,640]{2,1,0:T(8,128)(2,1)S(1)}, u32[]{:S(2)}, u32[]{:S(2)}) async-start(bf16[4,192,640]{2,1,0:T(8,128)(2,1)} %shard_map.52), calls=%async_computation | async-start | bytes 1966080 | tf_op jit(solution)/shard_map/all_to_all | solution.py:157
  10.2 0.7 copy-done.3
  10.9 3.5 %collective-permute-start = (bf16[208,640]{1,0:T(8,128)(2,1)S(1)}, bf16[208,640]{1,0:T(8,128)(2,1)S(1)}, u32[]{:S(2)}, u32[]{:S(2)}) collective-permute-start(bf16[208,640]{1,0:T(8,128)(2,1)S(1)} %shard_map.50.i0), channel_id=1, source_target_pairs={{0,64},{64,128},{128,192},{192,0},{1,65},{65,129},{129,193},{193,1... | collective-permute-start | bytes 798728 | tf_op jit(solution)/shard_map/ppermute | solution.py:26
  14.4 3.0 %collective-permute-start.1 = (bf16[208,640]{1,0:T(8,128)(2,1)S(1)}, bf16[208,640]{1,0:T(8,128)(2,1)S(1)}, u32[]{:S(2)}, u32[]{:S(2)}) collective-permute-start(bf16[208,640]{1,0:T(8,128)(2,1)S(1)} %shard_map.50.i0), channel_id=1, source_target_pairs={{0,128},{64,192},{128,0},{192,64},{1,129},{65,193},{129,1},{193,65... | collective-permute-start | bytes 798728 | tf_op jit(solution)/shard_map/ppermute | solution.py:26
  17.4 4.1 %collective-permute-start.2 = (bf16[208,640]{1,0:T(8,128)(2,1)S(1)}, bf16[208,640]{1,0:T(8,128)(2,1)S(1)}, u32[]{:S(2)}, u32[]{:S(2)}) collective-permute-start(bf16[208,640]{1,0:T(8,128)(2,1)S(1)} %shard_map.50.i0), channel_id=1, source_target_pairs={{0,192},{64,0},{128,64},{192,128},{1,193},{65,1},{129,65},{193,129... | collective-permute-start | bytes 798728 | tf_op jit(solution)/shard_map/ppermute | solution.py:26
  21.5 0.2 collective-permute-done.i1
  21.7 5.4 %collective-permute-done.1.i2 = bf16[208,640]{1,0:T(8,128)(2,1)S(1)} collective-permute-done((bf16[208,640]{1,0:T(8,128)(2,1)S(1)}, bf16[208,640]{1,0:T(8,128)(2,1)S(1)}, u32[]{:S(2)}, u32[]{:S(2)}) %collective-permute-start.1) | collective-permute-done | bytes 266272 | tf_op jit(solution)/shard_map/ppermute | solution.py:26
  27.2 3.6 %collective-permute-done.2.i3 = bf16[208,640]{1,0:T(8,128)(2,1)S(1)} collective-permute-done((bf16[208,640]{1,0:T(8,128)(2,1)S(1)}, bf16[208,640]{1,0:T(8,128)(2,1)S(1)}, u32[]{:S(2)}, u32[]{:S(2)}) %collective-permute-start.2) | collective-permute-done | bytes 266272 | tf_op jit(solution)/shard_map/ppermute | solution.py:26
  30.8 0.9 %shard_map.51 = (f32[192,640]{1,0:T(8,128)S(1)}, bf16[768,640]{1,0:T(8,128)(2,1)S(1)}, f32[1,768]{1,0:T(1,128)S(1)}, bf16[192,768]{1,0:T(8,128)(2,1)S(1)}) custom-call(bf16[208,640]{1,0:T(8,128)(2,1)S(1)} %shard_map.50.i0, bf16[208,640]{1,0:T(8,128)(2,1)S(1)} %collective-permute-done.i1, bf16[208,640]{1,0:T(8,128)(2,1)S(1)} %collective-permute-done.1.i2, ...), custom_call_target="tpu_custom_call" | custom-call | flops 377487360 | bytes 4194304 | tf_op jit(solution)/shard_map/pallas_call | solution.py:124
  31.8 3.4 %all-to-all-done.stack = bf16[4,192,640]{2,1,0:T(8,128)(2,1)S(1)} async-done(((bf16[4,192,640]{2,1,0:T(8,128)(2,1)}), bf16[4,192,640]{2,1,0:T(8,128)(2,1)S(1)}, u32[]{:S(2)}, u32[]{:S(2)}) %all-to-all-start) | async-done | bytes 983072 | tf_op jit(solution)/shard_map/all_to_all | solution.py:157
  35.1 3.1 %shard_map.53 = (bf16[4,192,640]{2,1,0:T(8,128)(2,1)}, bf16[576,768]{1,0:T(8,128)(2,1)S(1)}) custom-call(bf16[4,192,640]{2,1,0:T(8,128)(2,1)S(1)} %all-to-all-done.stack, bf16[768,640]{1,0:T(8,128)(2,1)S(1)} %get-tuple-element.13.images, f32[1,768]{1,0:T(1,128)S(1)} %get-tuple-element.14.labels), custom_call_target="tpu_custom_call" | custom-call | flops 1132462080 | bytes 4194304 | tf_op jit(solution)/shard_map/pallas_call | solution.py:124
  38.2 0.9 %copy-done.4 = bf16[576,768]{1,0:T(8,128)(2,1)} copy-done((bf16[576,768]{1,0:T(8,128)(2,1)}, bf16[576,768]{1,0:T(8,128)(2,1)S(1)}, u32[]{:S(2)}) %copy-start.4) | copy-done | bytes 884760
  39.2 4.2 %all-to-all-start.1 = ((bf16[4,192,640]{2,1,0:T(8,128)(2,1)}), bf16[4,192,640]{2,1,0:T(8,128)(2,1)S(1)}, u32[]{:S(2)}, u32[]{:S(2)}) async-start(bf16[4,192,640]{2,1,0:T(8,128)(2,1)} %get-tuple-element.15), calls=%async_computation.1 | async-start | bytes 1966080 | tf_op jit(solution)/shard_map/all_to_all | solution.py:175
  43.3 1.2 %copy-done.5 = bf16[576,768]{1,0:T(8,128)(2,1)S(1)} copy-done((bf16[576,768]{1,0:T(8,128)(2,1)S(1)}, bf16[576,768]{1,0:T(8,128)(2,1)}, u32[]{:S(2)}) %copy-start.5) | copy-done | bytes 884760
  44.5 1.4 %shard_map.54 = (f32[192,640]{1,0:T(8,128)S(1)}, bf16[192,640]{1,0:T(8,128)(2,1)S(1)}, bf16[192,640]{1,0:T(8,128)(2,1)S(1)}, bf16[192,640]{1,0:T(8,128)(2,1)S(1)}) custom-call(bf16[192,768]{1,0:T(8,128)(2,1)S(1)} %get-tuple-element.16.near, bf16[576,768]{1,0:T(8,128)(2,1)S(1)} %copy-done.5, bf16[192,640]{1,0:T(8,128)(2,1)S(1)} %copy-done.1, ...), custom_call_target="tpu_custom_call" | custom-call | flops 754974720 | bytes 4194304 | tf_op jit(solution)/shard_map/pallas_call | solution.py:124
  46.0 2.4 %collective-permute-start.3 = (bf16[192,640]{1,0:T(8,128)(2,1)S(1)}, bf16[192,640]{1,0:T(8,128)(2,1)S(1)}, u32[]{:S(2)}, u32[]{:S(2)}) collective-permute-start(bf16[192,640]{1,0:T(8,128)(2,1)S(1)} %get-tuple-element.19), channel_id=1, source_target_pairs={{0,192},{64,0},{128,64},{192,128},{1,193},{65,1},{129,65},{193,129... | collective-permute-start | bytes 737288 | tf_op jit(solution)/shard_map/ppermute | solution.py:26
  48.4 4.3 %collective-permute-start.4 = (bf16[192,640]{1,0:T(8,128)(2,1)S(1)}, bf16[192,640]{1,0:T(8,128)(2,1)S(1)}, u32[]{:S(2)}, u32[]{:S(2)}) collective-permute-start(bf16[192,640]{1,0:T(8,128)(2,1)S(1)} %get-tuple-element.20), channel_id=1, source_target_pairs={{0,128},{64,192},{128,0},{192,64},{1,129},{65,193},{129,1},{193,65... | collective-permute-start | bytes 737288 | tf_op jit(solution)/shard_map/ppermute | solution.py:26
  52.7 3.7 %collective-permute-start.5 = (bf16[192,640]{1,0:T(8,128)(2,1)S(1)}, bf16[192,640]{1,0:T(8,128)(2,1)S(1)}, u32[]{:S(2)}, u32[]{:S(2)}) collective-permute-start(bf16[192,640]{1,0:T(8,128)(2,1)S(1)} %get-tuple-element.21), channel_id=1, source_target_pairs={{0,64},{64,128},{128,192},{192,0},{1,65},{65,129},{129,193},{193,1... | collective-permute-start | bytes 737288 | tf_op jit(solution)/shard_map/ppermute | solution.py:26
  56.5 4.5 %collective-permute-done.4.x2 = bf16[192,640]{1,0:T(8,128)(2,1)S(1)} collective-permute-done((bf16[192,640]{1,0:T(8,128)(2,1)S(1)}, bf16[192,640]{1,0:T(8,128)(2,1)S(1)}, u32[]{:S(2)}, u32[]{:S(2)}) %collective-permute-start.4) | collective-permute-done | bytes 245792 | tf_op jit(solution)/shard_map/ppermute | solution.py:26
  61.0 2.8 %collective-permute-done.5.x3 = bf16[192,640]{1,0:T(8,128)(2,1)S(1)} collective-permute-done((bf16[192,640]{1,0:T(8,128)(2,1)S(1)}, bf16[192,640]{1,0:T(8,128)(2,1)S(1)}, u32[]{:S(2)}, u32[]{:S(2)}) %collective-permute-start.5) | collective-permute-done | bytes 245792 | tf_op jit(solution)/shard_map/ppermute | solution.py:26
  63.8 4.4 %all-to-all-done.1.parts = bf16[4,192,640]{2,1,0:T(8,128)(2,1)S(1)} async-done(((bf16[4,192,640]{2,1,0:T(8,128)(2,1)}), bf16[4,192,640]{2,1,0:T(8,128)(2,1)S(1)}, u32[]{:S(2)}, u32[]{:S(2)}) %all-to-all-start.1) | async-done | bytes 983072 | tf_op jit(solution)/shard_map/all_to_all | solution.py:175
  68.2 1.0 %shard_map.55 = (f32[192,640]{1,0:T(8,128)}, f32[192,640]{1,0:T(8,128)}) custom-call(f32[192,640]{1,0:T(8,128)S(1)} %get-tuple-element.12.own, bf16[4,192,640]{2,1,0:T(8,128)(2,1)S(1)} %all-to-all-done.1.parts, f32[192,640]{1,0:T(8,128)S(1)} %get-tuple-element.18.g0, bf16[192,640]{1,0:T(8,128)(2,1)S(1)} %collective-permute-done.3.x1, ...), custom_call_target="tpu_custom_call" | custom-call | bytes 4194304 | tf_op jit(solution)/shard_map/pallas_call | solution.py:124
  (10 shorter events, 0.0 us)
Async XLA Ops:
  0.6 0.9 %copy-start = (bf16[192,640]{1,0:T(8,128)(2,1)S(1)}, bf16[192,640]{1,0:T(8,128)(2,1)}, u32[]{:S(2)}) copy-start(bf16[192,640]{1,0:T(8,128)(2,1)} %texts.5) | copy-start | bytes 737284
  2.6 7.6 %copy-start.2 = (bf16[192,640]{1,0:T(8,128)(2,1)S(1)}, bf16[192,640]{1,0:T(8,128)(2,1)}, u32[]{:S(2)}) copy-start(bf16[192,640]{1,0:T(8,128)(2,1)} %images.1) | copy-start | bytes 737284
  2.6 32.5 %all-to-all-start = ((bf16[4,192,640]{2,1,0:T(8,128)(2,1)}), bf16[4,192,640]{2,1,0:T(8,128)(2,1)S(1)}, u32[]{:S(2)}, u32[]{:S(2)}) async-start(bf16[4,192,640]{2,1,0:T(8,128)(2,1)} %shard_map.52), calls=%async_computation | async-start | bytes 1966080 | tf_op jit(solution)/shard_map/all_to_all | solution.py:157
  10.2 0.7 copy-start.3
  10.8 20.0 %copy-start.1 = (bf16[192,640]{1,0:T(8,128)(2,1)S(1)}, bf16[192,640]{1,0:T(8,128)(2,1)}, u32[]{:S(2)}) copy-start(bf16[192,640]{1,0:T(8,128)(2,1)} %texts.5) | copy-start | bytes 737284
  10.9 10.9 %collective-permute-start = (bf16[208,640]{1,0:T(8,128)(2,1)S(1)}, bf16[208,640]{1,0:T(8,128)(2,1)S(1)}, u32[]{:S(2)}, u32[]{:S(2)}) collective-permute-start(bf16[208,640]{1,0:T(8,128)(2,1)S(1)} %shard_map.50.i0), channel_id=1, source_target_pairs={{0,64},{64,128},{128,192},{192,0},{1,65},{65,129},{129,193},{193,1... | collective-permute-start | bytes 798728 | tf_op jit(solution)/shard_map/ppermute | solution.py:26
  14.4 12.8 %collective-permute-start.1 = (bf16[208,640]{1,0:T(8,128)(2,1)S(1)}, bf16[208,640]{1,0:T(8,128)(2,1)S(1)}, u32[]{:S(2)}, u32[]{:S(2)}) collective-permute-start(bf16[208,640]{1,0:T(8,128)(2,1)S(1)} %shard_map.50.i0), channel_id=1, source_target_pairs={{0,128},{64,192},{128,0},{192,64},{1,129},{65,193},{129,1},{193,65... | collective-permute-start | bytes 798728 | tf_op jit(solution)/shard_map/ppermute | solution.py:26
  17.4 13.4 %collective-permute-start.2 = (bf16[208,640]{1,0:T(8,128)(2,1)S(1)}, bf16[208,640]{1,0:T(8,128)(2,1)S(1)}, u32[]{:S(2)}, u32[]{:S(2)}) collective-permute-start(bf16[208,640]{1,0:T(8,128)(2,1)S(1)} %shard_map.50.i0), channel_id=1, source_target_pairs={{0,192},{64,0},{128,64},{192,128},{1,193},{65,1},{129,65},{193,129... | collective-permute-start | bytes 798728 | tf_op jit(solution)/shard_map/ppermute | solution.py:26
  38.2 0.9 %copy-start.4 = (bf16[576,768]{1,0:T(8,128)(2,1)}, bf16[576,768]{1,0:T(8,128)(2,1)S(1)}, u32[]{:S(2)}) copy-start(bf16[576,768]{1,0:T(8,128)(2,1)S(1)} %get-tuple-element.17.coeff) | copy-start | bytes 2654212
  39.2 29.0 %all-to-all-start.1 = ((bf16[4,192,640]{2,1,0:T(8,128)(2,1)}), bf16[4,192,640]{2,1,0:T(8,128)(2,1)S(1)}, u32[]{:S(2)}, u32[]{:S(2)}) async-start(bf16[4,192,640]{2,1,0:T(8,128)(2,1)} %get-tuple-element.15), calls=%async_computation.1 | async-start | bytes 1966080 | tf_op jit(solution)/shard_map/all_to_all | solution.py:175
  43.3 1.2 %copy-start.5 = (bf16[576,768]{1,0:T(8,128)(2,1)S(1)}, bf16[576,768]{1,0:T(8,128)(2,1)}, u32[]{:S(2)}) copy-start(bf16[576,768]{1,0:T(8,128)(2,1)} %copy-done.4) | copy-start | bytes 2654212
  46.0 10.5 %collective-permute-start.3 = (bf16[192,640]{1,0:T(8,128)(2,1)S(1)}, bf16[192,640]{1,0:T(8,128)(2,1)S(1)}, u32[]{:S(2)}, u32[]{:S(2)}) collective-permute-start(bf16[192,640]{1,0:T(8,128)(2,1)S(1)} %get-tuple-element.19), channel_id=1, source_target_pairs={{0,192},{64,0},{128,64},{192,128},{1,193},{65,1},{129,65},{193,129... | collective-permute-start | bytes 737288 | tf_op jit(solution)/shard_map/ppermute | solution.py:26
  48.4 12.6 %collective-permute-start.4 = (bf16[192,640]{1,0:T(8,128)(2,1)S(1)}, bf16[192,640]{1,0:T(8,128)(2,1)S(1)}, u32[]{:S(2)}, u32[]{:S(2)}) collective-permute-start(bf16[192,640]{1,0:T(8,128)(2,1)S(1)} %get-tuple-element.20), channel_id=1, source_target_pairs={{0,128},{64,192},{128,0},{192,64},{1,129},{65,193},{129,1},{193,65... | collective-permute-start | bytes 737288 | tf_op jit(solution)/shard_map/ppermute | solution.py:26
  52.7 11.1 %collective-permute-start.5 = (bf16[192,640]{1,0:T(8,128)(2,1)S(1)}, bf16[192,640]{1,0:T(8,128)(2,1)S(1)}, u32[]{:S(2)}, u32[]{:S(2)}) collective-permute-start(bf16[192,640]{1,0:T(8,128)(2,1)S(1)} %get-tuple-element.21), channel_id=1, source_target_pairs={{0,64},{64,128},{128,192},{192,0},{1,65},{65,129},{129,193},{193,1... | collective-permute-start | bytes 737288 | tf_op jit(solution)/shard_map/ppermute | solution.py:26

commit v4 on v3

v4 whole, which is shorter than its diff:
```python
import functools

import jax
import jax.numpy as jnp
from jax import lax
from jax.experimental import pallas as pl
from jax.experimental.pallas import tpu as pltpu
from jax.sharding import Mesh, PartitionSpec as P

logit_scale = 25.0
logit_bias = -1.0
sides = 4
send_type = jnp.bfloat16
label_base = 64
log2_e = 1.4426950408889634
pad_rows = 16
chunks = 4

nt = (((1,), (1,)), ((), ()))
tn = (((0,), (0,)), ((), ()))
vmem = pl.BlockSpec(memory_space=pltpu.VMEM)
hbm = pl.BlockSpec(memory_space=pltpu.HBM)


def shifted(value, axis, steps):
    pairs = [(source, (source + steps) % sides) for source in range(sides)]
    return lax.ppermute(value, axis, pairs)


def together(*values):
    return lax.optimization_barrier(values)


def copies_kernel(texts, out, held, in_sems, out_sems):
    part = texts.shape[0] // chunks
    spans = [pl.ds(c * part, part) for c in range(chunks)]
    reads = [pltpu.make_async_copy(texts.at[span], held.at[span], in_sems.at[c]) for c, span in enumerate(spans)]
    for read in reads:
        read.start()
    writes = []
    for c, span in enumerate(spans):
        reads[c].wait()
        for k in range(sides):
            writes.append(pltpu.make_async_copy(held.at[span], out.at[k, span], out_sems.at[c, k]))
            writes[-1].start()
    for write in writes:
        write.wait()


def bundle_kernel(images, labels, out):
    rows, width = images.shape
    out[:rows, :] = images[...]
    value = labels[...]
    high = value // label_base
    low = value - high * label_base
    line = lax.broadcasted_iota(jnp.int32, (pad_rows, rows), 0)
    digits = jnp.where(line == 0, high, jnp.where(line == 1, low, 0))
    out[rows:, :rows] = digits.astype(jnp.float32).astype(jnp.bfloat16)
    out[rows:, rows:] = jnp.zeros((pad_rows, width - rows), jnp.bfloat16)


def coefficients(text_rows, images, labels, ids):
    dots = lax.dot_general(text_rows, images, nt, preferred_element_type=jnp.float32)
    sign = jnp.where(labels == ids, jnp.float32(-1.0), jnp.float32(1.0))
    power = (dots * (-logit_scale * log2_e) - logit_bias * log2_e) * sign
    return (sign * (1.0 / (1.0 + jnp.exp2(power)))).astype(jnp.bfloat16)


def text_ids(first, rows):
    line = lax.broadcasted_iota(jnp.int32, (rows, 1), 0)
    return (first * rows + line).astype(jnp.float32)


def near_kernel(scale, i0, i1, i2, i3, texts, own, images, labels, labs):
    rows = own.shape[0]
    for k, bundle in enumerate((i0, i1, i2, i3)):
        images[k * rows : (k + 1) * rows, :] = bundle[:rows, :]
        digits = bundle[rows:, :].astype(jnp.float32)
        labs[k : k + 1, :] = label_base * digits[0:1, :rows] + digits[1:2, :rows]
    labels[...] = jnp.concatenate([labs[k : k + 1, :] for k in range(sides)], axis=1)
    y, x = lax.axis_index("yh"), lax.axis_index("xx")
    c = coefficients(texts[...], images[...], labels[...], text_ids(y * sides + x, rows))
    own[...] = scale * jnp.dot(c, images[...], preferred_element_type=jnp.float32)


def far_kernel(scale, stack, images, labels, parts, texts, made, sems):
    rows = stack.shape[1]
    y, x = lax.axis_index("yh"), lax.axis_index("xx")
    owners = [lax.rem(y + n, sides) for n in range(1, sides)]
    for n, owner in enumerate(owners):
        texts[n * rows : (n + 1) * rows, :] = stack[owner]
    ids = jnp.concatenate([text_ids(owner * sides + x, rows) for owner in owners], axis=0)
    coeff = coefficients(texts[...], images[...], labels[...], ids)
    moves = []
    part = scale * jnp.dot(coeff, images[...], preferred_element_type=jnp.float32)
    for n, owner in enumerate(owners):
        made[n] = part[n * rows : (n + 1) * rows, :].astype(made.dtype)
        moves.append(pltpu.make_async_copy(made.at[n], parts.at[owner], sems.at[n]))
        moves[-1].start()
    for move in moves:
        move.wait()


def image_kernel(scale, images, labels, stack, g0, g1, g2, g3):
    rows = g0.shape[0]
    y, x = lax.axis_index("yh"), lax.axis_index("xx")
    value = None
    for n in range(sides):
        owner = lax.rem(y + n, sides)
        c = coefficients(stack[owner], images[...], labels[...], text_ids(owner * sides + x, rows))
        term = lax.dot_general(c, stack[owner], tn, preferred_element_type=jnp.float32)
        value = term if value is None else value + term
    for k, out in enumerate((g0, g1, g2, g3)):
        out[...] = (scale * value[k * rows : (k + 1) * rows, :]).astype(out.dtype)


def image_sum_kernel(g0, x1, x2, x3, image_grads):
    f32 = jnp.float32
    image_grads[...] = g0[...] + x1[...].astype(f32) + x2[...].astype(f32) + x3[...].astype(f32)


def text_sum_kernel(own, parts, text_grads):
    y = lax.axis_index("yh")
    total = own[...]
    for step in range(1, sides):
        total = total + parts[lax.rem(y + step, sides)].astype(jnp.float32)
    text_grads[...] = total


def call(kernel, shapes, scratch=(), flops=0, inputs=vmem, outputs=None, grant=48):
    def run(*operands):
        return pl.pallas_call(
            kernel,
            out_shape=shapes,
            in_specs=[inputs] * len(operands),
            out_specs=[vmem] * len(shapes) if outputs is None else outputs,
            scratch_shapes=list(scratch),
            compiler_params=pltpu.CompilerParams(vmem_limit_bytes=grant * 1024 * 1024),
            cost_estimate=pl.CostEstimate(flops=flops, bytes_accessed=4 << 20, transcendentals=0),
        )(*operands)

    return run


def on_device(image_embeddings, text_embeddings, pair_labels):
    rows, width = text_embeddings.shape
    scale = logit_scale / (sides * sides)
    f32 = jnp.float32
    block = (rows, width)
    every = sides * rows

    dots = 2 * rows * every * width
    half = jnp.bfloat16
    shape = jax.ShapeDtypeStruct

    (copies,) = call(
        copies_kernel,
        [shape((sides,) + block, half)],
        [pltpu.VMEM(block, half), pltpu.SemaphoreType.DMA((chunks,)), pltpu.SemaphoreType.DMA((chunks, sides))],
        inputs=hbm,
        outputs=[hbm],
        grant=60,
    )(text_embeddings)
    (bundle,) = call(bundle_kernel, [shape((rows + pad_rows, width), half)])(
        image_embeddings, pair_labels.reshape(1, rows)
    )
    stack = lax.all_to_all(copies, "yh", 0, 0)
    image_1 = shifted(bundle, "xx", 1)
    image_2 = shifted(bundle, "xx", 2)
    image_3 = shifted(bundle, "xx", -1)

    own, images, labels = call(
        functools.partial(near_kernel, scale),
        [shape(block, f32), shape((every, width), half), shape((1, every), f32)],
        [pltpu.VMEM((8, rows), f32)],
        2 * dots,
    )(bundle, image_1, image_2, image_3, text_embeddings)
    (parts,) = call(
        functools.partial(far_kernel, scale),
        [shape((sides,) + block, send_type)],
        [pltpu.VMEM(((sides - 1) * rows, width), half), pltpu.VMEM((sides - 1,) + block, send_type), pltpu.SemaphoreType.DMA((sides - 1,))],
        6 * dots,
        outputs=[hbm],
    )(stack, images, labels)
    parts = lax.all_to_all(parts, "yh", 0, 0)
    g0, g1, g2, g3 = call(
        functools.partial(image_kernel, scale),
        [shape(block, f32)] + [shape(block, send_type)] * 3,
        (),
        4 * dots,
    )(images, labels, stack)
    grad_1 = shifted(g1, "xx", -1)
    grad_2 = shifted(g2, "xx", 2)
    grad_3 = shifted(g3, "xx", 1)
    (image_grads,) = call(image_sum_kernel, [shape(block, f32)])(g0, grad_1, grad_2, grad_3)
    (text_grads,) = call(text_sum_kernel, [shape(block, f32)])(own, parts)
    return image_grads, text_grads


def solution(mesh):
    grid = Mesh(mesh.devices.reshape(sides, sides, -1), ("yh", "xx", "dp"))
    rows = P(("dp", "yh", "xx"), None)
    return jax.shard_map(
        on_device,
        mesh=grid,
        in_specs=(rows, rows, P(("dp", "yh", "xx"))),
        out_specs=(rows, rows),
        check_vma=False,
    )
```

time: 69.7 us -> 68.2 us (0.978)
  the two profiles are of different devices: /device:TPU:466 before, /device:TPU:16 now
where the time goes in v4:
time: 68.2 us; the launch traced here: 67.7 us
  starting transfers between devices  42.2 us (62%)
  waiting for transfers between devices  13.7 us (20%)
  Pallas kernels  10.4 us (15%)
  between operations  0.73 us (1%)
  local copies, waits for them, and re-layouts  0.69 us (1%)
    ppermute x6, starting transfers between devices, shifted(): return lax.ppermute(value, axis, pairs)  18.4 us
    all_to_all x1, starting transfers between devices, on_device(): stack = lax.all_to_all(copies, 'yh', 0, 0)  16.6 us
    ppermute x6, waiting for transfers between devices, shifted(): return lax.ppermute(value, axis, pairs)  13.7 us
    pallas_call x7, Pallas kernels, run(): pl.pallas_call(kernel, out_shape=shapes, in_specs=[inputs] * len(operands...  10.4 us
    all_to_all x1, starting transfers between devices, on_device(): parts = lax.all_to_all(parts, 'yh', 0, 0)  7.22 us
  transfers between devices with their start and end apart: 8, of which 5 were waited for; matrix products, arithmetic and copies ran while one was open for 0% of the time, Pallas kernels for 7%

profile of v4, /device:TPU:16, one launch (start us, length us, event | category | flops | bytes accessed | tf_op | source)
XLA Modules:
  0.0 67.7 jit_solution(5982047656451778464)
XLA Ops:
  0.6 2.0 %shard_map.52 = bf16[4,192,640]{2,1,0:T(8,128)(2,1)} custom-call(bf16[192,640]{1,0:T(8,128)(2,1)} %texts.3), custom_call_target="tpu_custom_call" | custom-call | bytes 4194304 | tf_op jit(solution)/shard_map/pallas_call | solution.py:132
  2.6 0.0 copy-start.1
  2.6 16.6 %all-to-all-start = ((bf16[4,192,640]{2,1,0:T(8,128)(2,1)}), bf16[4,192,640]{2,1,0:T(8,128)(2,1)S(1)}, u32[]{:S(2)}, u32[]{:S(2)}) async-start(bf16[4,192,640]{2,1,0:T(8,128)(2,1)} %shard_map.52), calls=%async_computation | async-start | bytes 1966080 | tf_op jit(solution)/shard_map/all_to_all | solution.py:167
  19.2 0.7 copy-done.2
  19.9 2.1 %collective-permute-start = (bf16[208,640]{1,0:T(8,128)(2,1)S(1)}, bf16[208,640]{1,0:T(8,128)(2,1)S(1)}, u32[]{:S(2)}, u32[]{:S(2)}) collective-permute-start(bf16[208,640]{1,0:T(8,128)(2,1)S(1)} %shard_map.50.i0), channel_id=1, source_target_pairs={{0,64},{64,128},{128,192},{192,0},{1,65},{65,129},{129,193},{193,1... | collective-permute-start | bytes 798728 | tf_op jit(solution)/shard_map/ppermute | solution.py:27
  22.0 1.9 %collective-permute-start.1 = (bf16[208,640]{1,0:T(8,128)(2,1)S(1)}, bf16[208,640]{1,0:T(8,128)(2,1)S(1)}, u32[]{:S(2)}, u32[]{:S(2)}) collective-permute-start(bf16[208,640]{1,0:T(8,128)(2,1)S(1)} %shard_map.50.i0), channel_id=1, source_target_pairs={{0,128},{64,192},{128,0},{192,64},{1,129},{65,193},{129,1},{193,65... | collective-permute-start | bytes 798728 | tf_op jit(solution)/shard_map/ppermute | solution.py:27
  23.9 5.1 %collective-permute-start.2 = (bf16[208,640]{1,0:T(8,128)(2,1)S(1)}, bf16[208,640]{1,0:T(8,128)(2,1)S(1)}, u32[]{:S(2)}, u32[]{:S(2)}) collective-permute-start(bf16[208,640]{1,0:T(8,128)(2,1)S(1)} %shard_map.50.i0), channel_id=1, source_target_pairs={{0,192},{64,0},{128,64},{192,128},{1,193},{65,1},{129,65},{193,129... | collective-permute-start | bytes 798728 | tf_op jit(solution)/shard_map/ppermute | solution.py:27
  29.1 3.4 %collective-permute-done.i1 = bf16[208,640]{1,0:T(8,128)(2,1)S(1)} collective-permute-done((bf16[208,640]{1,0:T(8,128)(2,1)S(1)}, bf16[208,640]{1,0:T(8,128)(2,1)S(1)}, u32[]{:S(2)}, u32[]{:S(2)}) %collective-permute-start) | collective-permute-done | bytes 266272 | tf_op jit(solution)/shard_map/ppermute | solution.py:27
  32.4 0.0 collective-permute-done.1.i2
  32.4 2.8 %collective-permute-done.2.i3 = bf16[208,640]{1,0:T(8,128)(2,1)S(1)} collective-permute-done((bf16[208,640]{1,0:T(8,128)(2,1)S(1)}, bf16[208,640]{1,0:T(8,128)(2,1)S(1)}, u32[]{:S(2)}, u32[]{:S(2)}) %collective-permute-start.2) | collective-permute-done | bytes 266272 | tf_op jit(solution)/shard_map/ppermute | solution.py:27
  35.2 0.9 %shard_map.51 = (f32[192,640]{1,0:T(8,128)S(1)}, bf16[768,640]{1,0:T(8,128)(2,1)S(1)}, f32[1,768]{1,0:T(1,128)S(1)}) custom-call(bf16[208,640]{1,0:T(8,128)(2,1)S(1)} %shard_map.50.i0, bf16[208,640]{1,0:T(8,128)(2,1)S(1)} %collective-permute-done.i1, bf16[208,640]{1,0:T(8,128)(2,1)S(1)} %collective-permute-done.1.i2, ...), custom_call_target="tpu_custom_call" | custom-call | flops 377487360 | bytes 4194304 | tf_op jit(solution)/shard_map/pallas_call | solution.py:132
  36.1 0.0 all-to-all-done.stack
  36.2 2.5 %shard_map.55 = bf16[4,192,640]{2,1,0:T(8,128)(2,1)} custom-call(bf16[4,192,640]{2,1,0:T(8,128)(2,1)S(1)} %all-to-all-done.stack, bf16[768,640]{1,0:T(8,128)(2,1)S(1)} %get-tuple-element.9.images, f32[1,768]{1,0:T(1,128)S(1)} %get-tuple-element.10.labels), custom_call_target="tpu_custom_call" | custom-call | flops 1132462080 | bytes 4194304 | tf_op jit(solution)/shard_map/pallas_call | solution.py:132
  38.7 7.2 %all-to-all-start.1 = ((bf16[4,192,640]{2,1,0:T(8,128)(2,1)}), bf16[4,192,640]{2,1,0:T(8,128)(2,1)S(1)}, u32[]{:S(2)}, u32[]{:S(2)}) async-start(bf16[4,192,640]{2,1,0:T(8,128)(2,1)} %shard_map.55), calls=%async_computation.1 | async-start | bytes 1966080 | tf_op jit(solution)/shard_map/all_to_all | solution.py:185
  45.9 3.2 %shard_map.53 = (f32[192,640]{1,0:T(8,128)S(1)}, bf16[192,640]{1,0:T(8,128)(2,1)S(1)}, bf16[192,640]{1,0:T(8,128)(2,1)S(1)}, bf16[192,640]{1,0:T(8,128)(2,1)S(1)}) custom-call(bf16[768,640]{1,0:T(8,128)(2,1)S(1)} %get-tuple-element.9.images, f32[1,768]{1,0:T(1,128)S(1)} %get-tuple-element.10.labels, bf16[4,192,640]{2,1,0:T(8,128)(2,1)S(1)} %all-to-all-done.stack), custom_call_target="tpu_custom_call" | custom-call | flops 754974720 | bytes 4194304 | tf_op jit(solution)/shard_map/pallas_call | solution.py:132
  49.1 4.6 %collective-permute-start.3 = (bf16[192,640]{1,0:T(8,128)(2,1)S(1)}, bf16[192,640]{1,0:T(8,128)(2,1)S(1)}, u32[]{:S(2)}, u32[]{:S(2)}) collective-permute-start(bf16[192,640]{1,0:T(8,128)(2,1)S(1)} %get-tuple-element.12), channel_id=1, source_target_pairs={{0,192},{64,0},{128,64},{192,128},{1,193},{65,1},{129,65},{193,129... | collective-permute-start | bytes 737288 | tf_op jit(solution)/shard_map/ppermute | solution.py:27
  53.7 2.4 %collective-permute-start.4 = (bf16[192,640]{1,0:T(8,128)(2,1)S(1)}, bf16[192,640]{1,0:T(8,128)(2,1)S(1)}, u32[]{:S(2)}, u32[]{:S(2)}) collective-permute-start(bf16[192,640]{1,0:T(8,128)(2,1)S(1)} %get-tuple-element.13), channel_id=1, source_target_pairs={{0,128},{64,192},{128,0},{192,64},{1,129},{65,193},{129,1},{193,65... | collective-permute-start | bytes 737288 | tf_op jit(solution)/shard_map/ppermute | solution.py:27
  56.1 2.3 %collective-permute-start.5 = (bf16[192,640]{1,0:T(8,128)(2,1)S(1)}, bf16[192,640]{1,0:T(8,128)(2,1)S(1)}, u32[]{:S(2)}, u32[]{:S(2)}) collective-permute-start(bf16[192,640]{1,0:T(8,128)(2,1)S(1)} %get-tuple-element.14), channel_id=1, source_target_pairs={{0,64},{64,128},{128,192},{192,0},{1,65},{65,129},{129,193},{193,1... | collective-permute-start | bytes 737288 | tf_op jit(solution)/shard_map/ppermute | solution.py:27
  58.4 1.8 %collective-permute-done.3.x1 = bf16[192,640]{1,0:T(8,128)(2,1)S(1)} collective-permute-done((bf16[192,640]{1,0:T(8,128)(2,1)S(1)}, bf16[192,640]{1,0:T(8,128)(2,1)S(1)}, u32[]{:S(2)}, u32[]{:S(2)}) %collective-permute-start.3) | collective-permute-done | bytes 245792 | tf_op jit(solution)/shard_map/ppermute | solution.py:27
  60.2 3.1 %collective-permute-done.4.x2 = bf16[192,640]{1,0:T(8,128)(2,1)S(1)} collective-permute-done((bf16[192,640]{1,0:T(8,128)(2,1)S(1)}, bf16[192,640]{1,0:T(8,128)(2,1)S(1)}, u32[]{:S(2)}, u32[]{:S(2)}) %collective-permute-start.4) | collective-permute-done | bytes 245792 | tf_op jit(solution)/shard_map/ppermute | solution.py:27
  63.3 2.6 %collective-permute-done.5.x3 = bf16[192,640]{1,0:T(8,128)(2,1)S(1)} collective-permute-done((bf16[192,640]{1,0:T(8,128)(2,1)S(1)}, bf16[192,640]{1,0:T(8,128)(2,1)S(1)}, u32[]{:S(2)}, u32[]{:S(2)}) %collective-permute-start.5) | collective-permute-done | bytes 245792 | tf_op jit(solution)/shard_map/ppermute | solution.py:27
  65.9 0.9 %shard_map.54 = f32[192,640]{1,0:T(8,128)} custom-call(f32[192,640]{1,0:T(8,128)S(1)} %get-tuple-element.11.g0, bf16[192,640]{1,0:T(8,128)(2,1)S(1)} %collective-permute-done.3.x1, bf16[192,640]{1,0:T(8,128)(2,1)S(1)} %collective-permute-done.4.x2, bf16[192,640]{1,0:T(8,128)(2,1)S(1)} %collective-permute-done.5.x3), custom_call_target="tpu_custom_call" | custom-call | bytes 4194304 | tf_op jit(solution)/shard_map/pallas_call | solution.py:132
  66.8 0.0 all-to-all-done.1.parts
  66.8 0.9 %shard_map.56 = f32[192,640]{1,0:T(8,128)} custom-call(f32[192,640]{1,0:T(8,128)S(1)} %get-tuple-element.15.own, bf16[4,192,640]{2,1,0:T(8,128)(2,1)S(1)} %all-to-all-done.1.parts), custom_call_target="tpu_custom_call" | custom-call | bytes 4194304 | tf_op jit(solution)/shard_map/pallas_call | solution.py:132
  (5 shorter events, 0.0 us)
Async XLA Ops:
  2.6 16.6 %copy-start.1 = (bf16[192,640]{1,0:T(8,128)(2,1)S(1)}, bf16[192,640]{1,0:T(8,128)(2,1)}, u32[]{:S(2)}) copy-start(bf16[192,640]{1,0:T(8,128)(2,1)} %images.1) | copy-start | bytes 737284
  2.6 33.5 %all-to-all-start = ((bf16[4,192,640]{2,1,0:T(8,128)(2,1)}), bf16[4,192,640]{2,1,0:T(8,128)(2,1)S(1)}, u32[]{:S(2)}, u32[]{:S(2)}) async-start(bf16[4,192,640]{2,1,0:T(8,128)(2,1)} %shard_map.52), calls=%async_computation | async-start | bytes 1966080 | tf_op jit(solution)/shard_map/all_to_all | solution.py:167
  19.2 0.7 %copy-start.2 = (s32[192]{0:T(256)S(1)}, s32[192]{0:T(256)}, u32[]{:S(2)}) copy-start(s32[192]{0:T(256)} %param.5) | copy-start | bytes 2308
  19.9 15.3 %copy-start = (bf16[192,640]{1,0:T(8,128)(2,1)S(1)}, bf16[192,640]{1,0:T(8,128)(2,1)}, u32[]{:S(2)}) copy-start(bf16[192,640]{1,0:T(8,128)(2,1)} %texts.3) | copy-start | bytes 737284
  19.9 12.5 %collective-permute-start = (bf16[208,640]{1,0:T(8,128)(2,1)S(1)}, bf16[208,640]{1,0:T(8,128)(2,1)S(1)}, u32[]{:S(2)}, u32[]{:S(2)}) collective-permute-start(bf16[208,640]{1,0:T(8,128)(2,1)S(1)} %shard_map.50.i0), channel_id=1, source_target_pairs={{0,64},{64,128},{128,192},{192,0},{1,65},{65,129},{129,193},{193,1... | collective-permute-start | bytes 798728 | tf_op jit(solution)/shard_map/ppermute | solution.py:27
  22.0 10.4 %collective-permute-start.1 = (bf16[208,640]{1,0:T(8,128)(2,1)S(1)}, bf16[208,640]{1,0:T(8,128)(2,1)S(1)}, u32[]{:S(2)}, u32[]{:S(2)}) collective-permute-start(bf16[208,640]{1,0:T(8,128)(2,1)S(1)} %shard_map.50.i0), channel_id=1, source_target_pairs={{0,128},{64,192},{128,0},{192,64},{1,129},{65,193},{129,1},{193,65... | collective-permute-start | bytes 798728 | tf_op jit(solution)/shard_map/ppermute | solution.py:27
  23.9 11.3 %collective-permute-start.2 = (bf16[208,640]{1,0:T(8,128)(2,1)S(1)}, bf16[208,640]{1,0:T(8,128)(2,1)S(1)}, u32[]{:S(2)}, u32[]{:S(2)}) collective-permute-start(bf16[208,640]{1,0:T(8,128)(2,1)S(1)} %shard_map.50.i0), channel_id=1, source_target_pairs={{0,192},{64,0},{128,64},{192,128},{1,193},{65,1},{129,65},{193,129... | collective-permute-start | bytes 798728 | tf_op jit(solution)/shard_map/ppermute | solution.py:27
  38.7 28.1 %all-to-all-start.1 = ((bf16[4,192,640]{2,1,0:T(8,128)(2,1)}), bf16[4,192,640]{2,1,0:T(8,128)(2,1)S(1)}, u32[]{:S(2)}, u32[]{:S(2)}) async-start(bf16[4,192,640]{2,1,0:T(8,128)(2,1)} %shard_map.55), calls=%async_computation.1 | async-start | bytes 1966080 | tf_op jit(solution)/shard_map/all_to_all | solution.py:185
  49.1 11.1 %collective-permute-start.3 = (bf16[192,640]{1,0:T(8,128)(2,1)S(1)}, bf16[192,640]{1,0:T(8,128)(2,1)S(1)}, u32[]{:S(2)}, u32[]{:S(2)}) collective-permute-start(bf16[192,640]{1,0:T(8,128)(2,1)S(1)} %get-tuple-element.12), channel_id=1, source_target_pairs={{0,192},{64,0},{128,64},{192,128},{1,193},{65,1},{129,65},{193,129... | collective-permute-start | bytes 737288 | tf_op jit(solution)/shard_map/ppermute | solution.py:27
  53.7 9.6 %collective-permute-start.4 = (bf16[192,640]{1,0:T(8,128)(2,1)S(1)}, bf16[192,640]{1,0:T(8,128)(2,1)S(1)}, u32[]{:S(2)}, u32[]{:S(2)}) collective-permute-start(bf16[192,640]{1,0:T(8,128)(2,1)S(1)} %get-tuple-element.13), channel_id=1, source_target_pairs={{0,128},{64,192},{128,0},{192,64},{1,129},{65,193},{129,1},{193,65... | collective-permute-start | bytes 737288 | tf_op jit(solution)/shard_map/ppermute | solution.py:27
  56.1 9.8 %collective-permute-start.5 = (bf16[192,640]{1,0:T(8,128)(2,1)S(1)}, bf16[192,640]{1,0:T(8,128)(2,1)S(1)}, u32[]{:S(2)}, u32[]{:S(2)}) collective-permute-start(bf16[192,640]{1,0:T(8,128)(2,1)S(1)} %get-tuple-element.14), channel_id=1, source_target_pairs={{0,64},{64,128},{128,192},{192,0},{1,65},{65,129},{129,193},{193,1... | collective-permute-start | bytes 737288 | tf_op jit(solution)/shard_map/ppermute | solution.py:27

commit v5 on v4

--- a/solution.py
+++ b/solution.py
@@ -103,28 +103,34 @@
 
 def image_kernel(scale, images, labels, stack, g0, g1, g2, g3):
     rows = g0.shape[0]
-    y, x = lax.axis_index("yh"), lax.axis_index("xx")
-    value = None
-    for n in range(sides):
-        owner = lax.rem(y + n, sides)
-        c = coefficients(stack[owner], images[...], labels[...], text_ids(owner * sides + x, rows))
-        term = lax.dot_general(c, stack[owner], tn, preferred_element_type=jnp.float32)
-        value = term if value is None else value + term
+    x = lax.axis_index("xx")
+    ids = jnp.concatenate([text_ids(n * sides + x, rows) for n in range(sides)], axis=0)
+    texts = stack[...].reshape(sides * rows, stack.shape[2])
+    c = coefficients(texts, images[...], labels[...], ids)
+    value = scale * lax.dot_general(c, texts, tn, preferred_element_type=jnp.float32)
     for k, out in enumerate((g0, g1, g2, g3)):
-        out[...] = (scale * value[k * rows : (k + 1) * rows, :]).astype(out.dtype)
-
-
-def image_sum_kernel(g0, x1, x2, x3, image_grads):
+        out[...] = value[k * rows : (k + 1) * rows, :].astype(out.dtype)
+
+
+def image_sum_kernel(g0, x1, x3, x2, image_grads):
     f32 = jnp.float32
     image_grads[...] = g0[...] + x1[...].astype(f32) + x2[...].astype(f32) + x3[...].astype(f32)
 
 
-def text_sum_kernel(own, parts, text_grads):
+def text_sum_kernel(own, parts, text_grads, held, sems):
     y = lax.axis_index("yh")
-    total = own[...]
-    for step in range(1, sides):
-        total = total + parts[lax.rem(y + step, sides)].astype(jnp.float32)
-    text_grads[...] = total
+    part = own.shape[0] // chunks
+    moves = []
+    for c in range(chunks):
+        span = pl.ds(c * part, part)
+        total = own[span, :]
+        for step in range(1, sides):
+            total = total + parts[lax.rem(y + step, sides), span, :].astype(jnp.float32)
+        held[span, :] = total
+        moves.append(pltpu.make_async_copy(held.at[span], text_grads.at[span], sems.at[c]))
+        moves[-1].start()
+    for move in moves:
+        move.wait()
 
 
 def call(kernel, shapes, scratch=(), flops=0, inputs=vmem, outputs=None, grant=48):
@@ -192,8 +198,13 @@
     grad_1 = shifted(g1, "xx", -1)
     grad_2 = shifted(g2, "xx", 2)
     grad_3 = shifted(g3, "xx", 1)
-    (image_grads,) = call(image_sum_kernel, [shape(block, f32)])(g0, grad_1, grad_2, grad_3)
-    (text_grads,) = call(text_sum_kernel, [shape(block, f32)])(own, parts)
+    (image_grads,) = call(image_sum_kernel, [shape(block, f32)])(g0, grad_1, grad_3, grad_2)
+    (text_grads,) = call(
+        text_sum_kernel,
+        [shape(block, f32)],
+        [pltpu.VMEM(block, f32), pltpu.SemaphoreType.DMA((chunks,))],
+        outputs=[hbm],
+    )(own, parts)
     return image_grads, text_grads
 
 

time: 68.2 us -> 68.1 us (level)
  the two profiles are of different devices: /device:TPU:16 before, /device:TPU:786 now
where the time goes in v5:
time: 68.1 us; the launch traced here: 67.6 us
  starting transfers between devices  33.5 us (49%)
  waiting for transfers between devices  22.9 us (34%)
  Pallas kernels  9.82 us (14%)
  between operations  0.73 us (1%)
  local copies, waits for them, and re-layouts  0.69 us (1%)
    ppermute x6, starting transfers between devices, shifted(): return lax.ppermute(value, axis, pairs)  21.7 us
    ppermute x6, waiting for transfers between devices, shifted(): return lax.ppermute(value, axis, pairs)  14 us
    pallas_call x7, Pallas kernels, run(): pl.pallas_call(kernel, out_shape=shapes, in_specs=[inputs] * len(operands...  9.82 us
    all_to_all x1, starting transfers between devices, on_device(): stack = lax.all_to_all(copies, 'yh', 0, 0)  7.57 us
    all_to_all x1, waiting for transfers between devices, on_device(): parts = lax.all_to_all(parts, 'yh', 0, 0)  5.54 us
    all_to_all x1, starting transfers between devices, on_device(): parts = lax.all_to_all(parts, 'yh', 0, 0)  4.2 us
    all_to_all x1, waiting for transfers between devices, on_device(): stack = lax.all_to_all(copies, 'yh', 0, 0)  3.38 us
  transfers between devices with their start and end apart: 8, of which 7 were waited for; matrix products, arithmetic and copies ran while one was open for 0% of the time, Pallas kernels for 7%

profile of v5, /device:TPU:786, one launch (start us, length us, event | category | flops | bytes accessed | tf_op | source)
XLA Modules:
  0.0 67.6 jit_solution(6672588673722588785)
XLA Ops:
  0.6 2.0 %shard_map.52 = bf16[4,192,640]{2,1,0:T(8,128)(2,1)} custom-call(bf16[192,640]{1,0:T(8,128)(2,1)} %texts.3), custom_call_target="tpu_custom_call" | custom-call | bytes 4194304 | tf_op jit(solution)/shard_map/pallas_call | solution.py:138
  2.6 0.0 copy-start.1
  2.6 7.6 %all-to-all-start = ((bf16[4,192,640]{2,1,0:T(8,128)(2,1)}), bf16[4,192,640]{2,1,0:T(8,128)(2,1)S(1)}, u32[]{:S(2)}, u32[]{:S(2)}) async-start(bf16[4,192,640]{2,1,0:T(8,128)(2,1)} %shard_map.52), calls=%async_computation | async-start | bytes 1966080 | tf_op jit(solution)/shard_map/all_to_all | solution.py:173
  10.2 0.7 copy-done.2
  10.9 3.5 %collective-permute-start = (bf16[208,640]{1,0:T(8,128)(2,1)S(1)}, bf16[208,640]{1,0:T(8,128)(2,1)S(1)}, u32[]{:S(2)}, u32[]{:S(2)}) collective-permute-start(bf16[208,640]{1,0:T(8,128)(2,1)S(1)} %shard_map.50.i0), channel_id=1, source_target_pairs={{0,64},{64,128},{128,192},{192,0},{1,65},{65,129},{129,193},{193,1... | collective-permute-start | bytes 798728 | tf_op jit(solution)/shard_map/ppermute | solution.py:27
  14.4 3.0 %collective-permute-start.1 = (bf16[208,640]{1,0:T(8,128)(2,1)S(1)}, bf16[208,640]{1,0:T(8,128)(2,1)S(1)}, u32[]{:S(2)}, u32[]{:S(2)}) collective-permute-start(bf16[208,640]{1,0:T(8,128)(2,1)S(1)} %shard_map.50.i0), channel_id=1, source_target_pairs={{0,128},{64,192},{128,0},{192,64},{1,129},{65,193},{129,1},{193,65... | collective-permute-start | bytes 798728 | tf_op jit(solution)/shard_map/ppermute | solution.py:27
  17.5 4.1 %collective-permute-start.2 = (bf16[208,640]{1,0:T(8,128)(2,1)S(1)}, bf16[208,640]{1,0:T(8,128)(2,1)S(1)}, u32[]{:S(2)}, u32[]{:S(2)}) collective-permute-start(bf16[208,640]{1,0:T(8,128)(2,1)S(1)} %shard_map.50.i0), channel_id=1, source_target_pairs={{0,192},{64,0},{128,64},{192,128},{1,193},{65,1},{129,65},{193,129... | collective-permute-start | bytes 798728 | tf_op jit(solution)/shard_map/ppermute | solution.py:27
  21.5 0.2 collective-permute-done.i1
  21.8 5.4 %collective-permute-done.1.i2 = bf16[208,640]{1,0:T(8,128)(2,1)S(1)} collective-permute-done((bf16[208,640]{1,0:T(8,128)(2,1)S(1)}, bf16[208,640]{1,0:T(8,128)(2,1)S(1)}, u32[]{:S(2)}, u32[]{:S(2)}) %collective-permute-start.1) | collective-permute-done | bytes 266272 | tf_op jit(solution)/shard_map/ppermute | solution.py:27
  27.2 3.6 %collective-permute-done.2.i3 = bf16[208,640]{1,0:T(8,128)(2,1)S(1)} collective-permute-done((bf16[208,640]{1,0:T(8,128)(2,1)S(1)}, bf16[208,640]{1,0:T(8,128)(2,1)S(1)}, u32[]{:S(2)}, u32[]{:S(2)}) %collective-permute-start.2) | collective-permute-done | bytes 266272 | tf_op jit(solution)/shard_map/ppermute | solution.py:27
  30.8 0.9 %shard_map.51 = (f32[192,640]{1,0:T(8,128)S(1)}, bf16[768,640]{1,0:T(8,128)(2,1)S(1)}, f32[1,768]{1,0:T(1,128)S(1)}) custom-call(bf16[208,640]{1,0:T(8,128)(2,1)S(1)} %shard_map.50.i0, bf16[208,640]{1,0:T(8,128)(2,1)S(1)} %collective-permute-done.i1, bf16[208,640]{1,0:T(8,128)(2,1)S(1)} %collective-permute-done.1.i2, ...), custom_call_target="tpu_custom_call" | custom-call | flops 377487360 | bytes 4194304 | tf_op jit(solution)/shard_map/pallas_call | solution.py:138
  31.8 3.4 %all-to-all-done.stack = bf16[4,192,640]{2,1,0:T(8,128)(2,1)S(1)} async-done(((bf16[4,192,640]{2,1,0:T(8,128)(2,1)}), bf16[4,192,640]{2,1,0:T(8,128)(2,1)S(1)}, u32[]{:S(2)}, u32[]{:S(2)}) %all-to-all-start) | async-done | bytes 983072 | tf_op jit(solution)/shard_map/all_to_all | solution.py:173
  35.2 2.5 %shard_map.55 = bf16[4,192,640]{2,1,0:T(8,128)(2,1)} custom-call(bf16[4,192,640]{2,1,0:T(8,128)(2,1)S(1)} %all-to-all-done.stack, bf16[768,640]{1,0:T(8,128)(2,1)S(1)} %get-tuple-element.9.images, f32[1,768]{1,0:T(1,128)S(1)} %get-tuple-element.10.labels), custom_call_target="tpu_custom_call" | custom-call | flops 1132462080 | bytes 4194304 | tf_op jit(solution)/shard_map/pallas_call | solution.py:138
  37.7 4.2 %all-to-all-start.1 = ((bf16[4,192,640]{2,1,0:T(8,128)(2,1)}), bf16[4,192,640]{2,1,0:T(8,128)(2,1)S(1)}, u32[]{:S(2)}, u32[]{:S(2)}) async-start(bf16[4,192,640]{2,1,0:T(8,128)(2,1)} %shard_map.55), calls=%async_computation.1 | async-start | bytes 1966080 | tf_op jit(solution)/shard_map/all_to_all | solution.py:191
  41.9 2.6 %shard_map.53 = (f32[192,640]{1,0:T(8,128)S(1)}, bf16[192,640]{1,0:T(8,128)(2,1)S(1)}, bf16[192,640]{1,0:T(8,128)(2,1)S(1)}, bf16[192,640]{1,0:T(8,128)(2,1)S(1)}) custom-call(bf16[768,640]{1,0:T(8,128)(2,1)S(1)} %get-tuple-element.9.images, f32[1,768]{1,0:T(1,128)S(1)} %get-tuple-element.10.labels, bf16[4,192,640]{2,1,0:T(8,128)(2,1)S(1)} %all-to-all-done.stack), custom_call_target="tpu_custom_call" | custom-call | flops 754974720 | bytes 4194304 | tf_op jit(solution)/shard_map/pallas_call | solution.py:138
  44.6 2.4 %collective-permute-start.3 = (bf16[192,640]{1,0:T(8,128)(2,1)S(1)}, bf16[192,640]{1,0:T(8,128)(2,1)S(1)}, u32[]{:S(2)}, u32[]{:S(2)}) collective-permute-start(bf16[192,640]{1,0:T(8,128)(2,1)S(1)} %get-tuple-element.12), channel_id=1, source_target_pairs={{0,192},{64,0},{128,64},{192,128},{1,193},{65,1},{129,65},{193,129... | collective-permute-start | bytes 737288 | tf_op jit(solution)/shard_map/ppermute | solution.py:27
  47.0 3.4 %collective-permute-start.4 = (bf16[192,640]{1,0:T(8,128)(2,1)S(1)}, bf16[192,640]{1,0:T(8,128)(2,1)S(1)}, u32[]{:S(2)}, u32[]{:S(2)}) collective-permute-start(bf16[192,640]{1,0:T(8,128)(2,1)S(1)} %get-tuple-element.13), channel_id=1, source_target_pairs={{0,64},{64,128},{128,192},{192,0},{1,65},{65,129},{129,193},{193,1... | collective-permute-start | bytes 737288 | tf_op jit(solution)/shard_map/ppermute | solution.py:27
  50.4 5.2 %collective-permute-start.5 = (bf16[192,640]{1,0:T(8,128)(2,1)S(1)}, bf16[192,640]{1,0:T(8,128)(2,1)S(1)}, u32[]{:S(2)}, u32[]{:S(2)}) collective-permute-start(bf16[192,640]{1,0:T(8,128)(2,1)S(1)} %get-tuple-element.14), channel_id=1, source_target_pairs={{0,128},{64,192},{128,0},{192,64},{1,129},{65,193},{129,1},{193,65... | collective-permute-start | bytes 737288 | tf_op jit(solution)/shard_map/ppermute | solution.py:27
  55.7 0.0 collective-permute-done.3.x1
  55.7 2.5 %collective-permute-done.4.x3 = bf16[192,640]{1,0:T(8,128)(2,1)S(1)} collective-permute-done((bf16[192,640]{1,0:T(8,128)(2,1)S(1)}, bf16[192,640]{1,0:T(8,128)(2,1)S(1)}, u32[]{:S(2)}, u32[]{:S(2)}) %collective-permute-start.4) | collective-permute-done | bytes 245792 | tf_op jit(solution)/shard_map/ppermute | solution.py:27
  58.2 2.1 %collective-permute-done.5.x2 = bf16[192,640]{1,0:T(8,128)(2,1)S(1)} collective-permute-done((bf16[192,640]{1,0:T(8,128)(2,1)S(1)}, bf16[192,640]{1,0:T(8,128)(2,1)S(1)}, u32[]{:S(2)}, u32[]{:S(2)}) %collective-permute-start.5) | collective-permute-done | bytes 245792 | tf_op jit(solution)/shard_map/ppermute | solution.py:27
  60.3 0.9 %shard_map.54 = f32[192,640]{1,0:T(8,128)} custom-call(f32[192,640]{1,0:T(8,128)S(1)} %get-tuple-element.11.g0, bf16[192,640]{1,0:T(8,128)(2,1)S(1)} %collective-permute-done.3.x1, bf16[192,640]{1,0:T(8,128)(2,1)S(1)} %collective-permute-done.4.x3, bf16[192,640]{1,0:T(8,128)(2,1)S(1)} %collective-permute-done.5.x2), custom_call_target="tpu_custom_call" | custom-call | bytes 4194304 | tf_op jit(solution)/shard_map/pallas_call | solution.py:138
  61.2 5.5 %all-to-all-done.1.parts = bf16[4,192,640]{2,1,0:T(8,128)(2,1)S(1)} async-done(((bf16[4,192,640]{2,1,0:T(8,128)(2,1)}), bf16[4,192,640]{2,1,0:T(8,128)(2,1)S(1)}, u32[]{:S(2)}, u32[]{:S(2)}) %all-to-all-start.1) | async-done | bytes 983072 | tf_op jit(solution)/shard_map/all_to_all | solution.py:191
  66.7 0.8 %shard_map.56 = f32[192,640]{1,0:T(8,128)} custom-call(f32[192,640]{1,0:T(8,128)S(1)} %get-tuple-element.15.own, bf16[4,192,640]{2,1,0:T(8,128)(2,1)S(1)} %all-to-all-done.1.parts), custom_call_target="tpu_custom_call" | custom-call | bytes 4194304 | tf_op jit(solution)/shard_map/pallas_call | solution.py:138
  (5 shorter events, 0.0 us)
Async XLA Ops:
  2.6 7.6 %copy-start.1 = (bf16[192,640]{1,0:T(8,128)(2,1)S(1)}, bf16[192,640]{1,0:T(8,128)(2,1)}, u32[]{:S(2)}) copy-start(bf16[192,640]{1,0:T(8,128)(2,1)} %images.1) | copy-start | bytes 737284
  2.6 32.5 %all-to-all-start = ((bf16[4,192,640]{2,1,0:T(8,128)(2,1)}), bf16[4,192,640]{2,1,0:T(8,128)(2,1)S(1)}, u32[]{:S(2)}, u32[]{:S(2)}) async-start(bf16[4,192,640]{2,1,0:T(8,128)(2,1)} %shard_map.52), calls=%async_computation | async-start | bytes 1966080 | tf_op jit(solution)/shard_map/all_to_all | solution.py:173
  10.2 0.7 %copy-start.2 = (s32[192]{0:T(256)S(1)}, s32[192]{0:T(256)}, u32[]{:S(2)}) copy-start(s32[192]{0:T(256)} %param.5) | copy-start | bytes 2308
  10.9 20.0 %copy-start = (bf16[192,640]{1,0:T(8,128)(2,1)S(1)}, bf16[192,640]{1,0:T(8,128)(2,1)}, u32[]{:S(2)}) copy-start(bf16[192,640]{1,0:T(8,128)(2,1)} %texts.3) | copy-start | bytes 737284
  10.9 10.9 %collective-permute-start = (bf16[208,640]{1,0:T(8,128)(2,1)S(1)}, bf16[208,640]{1,0:T(8,128)(2,1)S(1)}, u32[]{:S(2)}, u32[]{:S(2)}) collective-permute-start(bf16[208,640]{1,0:T(8,128)(2,1)S(1)} %shard_map.50.i0), channel_id=1, source_target_pairs={{0,64},{64,128},{128,192},{192,0},{1,65},{65,129},{129,193},{193,1... | collective-permute-start | bytes 798728 | tf_op jit(solution)/shard_map/ppermute | solution.py:27
  14.4 12.8 %collective-permute-start.1 = (bf16[208,640]{1,0:T(8,128)(2,1)S(1)}, bf16[208,640]{1,0:T(8,128)(2,1)S(1)}, u32[]{:S(2)}, u32[]{:S(2)}) collective-permute-start(bf16[208,640]{1,0:T(8,128)(2,1)S(1)} %shard_map.50.i0), channel_id=1, source_target_pairs={{0,128},{64,192},{128,0},{192,64},{1,129},{65,193},{129,1},{193,65... | collective-permute-start | bytes 798728 | tf_op jit(solution)/shard_map/ppermute | solution.py:27
  17.5 13.4 %collective-permute-start.2 = (bf16[208,640]{1,0:T(8,128)(2,1)S(1)}, bf16[208,640]{1,0:T(8,128)(2,1)S(1)}, u32[]{:S(2)}, u32[]{:S(2)}) collective-permute-start(bf16[208,640]{1,0:T(8,128)(2,1)S(1)} %shard_map.50.i0), channel_id=1, source_target_pairs={{0,192},{64,0},{128,64},{192,128},{1,193},{65,1},{129,65},{193,129... | collective-permute-start | bytes 798728 | tf_op jit(solution)/shard_map/ppermute | solution.py:27
  37.7 29.1 %all-to-all-start.1 = ((bf16[4,192,640]{2,1,0:T(8,128)(2,1)}), bf16[4,192,640]{2,1,0:T(8,128)(2,1)S(1)}, u32[]{:S(2)}, u32[]{:S(2)}) async-start(bf16[4,192,640]{2,1,0:T(8,128)(2,1)} %shard_map.55), calls=%async_computation.1 | async-start | bytes 1966080 | tf_op jit(solution)/shard_map/all_to_all | solution.py:191
  44.6 11.1 %collective-permute-start.3 = (bf16[192,640]{1,0:T(8,128)(2,1)S(1)}, bf16[192,640]{1,0:T(8,128)(2,1)S(1)}, u32[]{:S(2)}, u32[]{:S(2)}) collective-permute-start(bf16[192,640]{1,0:T(8,128)(2,1)S(1)} %get-tuple-element.12), channel_id=1, source_target_pairs={{0,192},{64,0},{128,64},{192,128},{1,193},{65,1},{129,65},{193,129... | collective-permute-start | bytes 737288 | tf_op jit(solution)/shard_map/ppermute | solution.py:27
  47.0 11.2 %collective-permute-start.4 = (bf16[192,640]{1,0:T(8,128)(2,1)S(1)}, bf16[192,640]{1,0:T(8,128)(2,1)S(1)}, u32[]{:S(2)}, u32[]{:S(2)}) collective-permute-start(bf16[192,640]{1,0:T(8,128)(2,1)S(1)} %get-tuple-element.13), channel_id=1, source_target_pairs={{0,64},{64,128},{128,192},{192,0},{1,65},{65,129},{129,193},{193,1... | collective-permute-start | bytes 737288 | tf_op jit(solution)/shard_map/ppermute | solution.py:27
  50.4 9.9 %collective-permute-start.5 = (bf16[192,640]{1,0:T(8,128)(2,1)S(1)}, bf16[192,640]{1,0:T(8,128)(2,1)S(1)}, u32[]{:S(2)}, u32[]{:S(2)}) collective-permute-start(bf16[192,640]{1,0:T(8,128)(2,1)S(1)} %get-tuple-element.14), channel_id=1, source_target_pairs={{0,128},{64,192},{128,0},{192,64},{1,129},{65,193},{129,1},{193,65... | collective-permute-start | bytes 737288 | tf_op jit(solution)/shard_map/ppermute | solution.py:27
